TPU v7x, 32 devices: a whole 2x2x4 slice. The times are simulated.
32 devices in a mesh: group: 2 (over x), tile: 8 (over z, y), draw: 2 (over core).
Axes of the slice: x: 2, y: 2, z: 4, core: 2. Of those that a mesh axis runs over, the one named last changes fastest.
Arguments:
- inputs: bfloat16 [4, 32, 270, 256], P(('group', 'draw'), 'tile'), parts along dimension 0, may hold values from -6 to 6
- land_mask: int32 [32, 270], P('tile'), may hold values 0 or 1
- kernel: float32 [7, 7, 256], replicated, may hold values from -0.875 to 0.875
- conv_bias: float32 [256], replicated, may hold values from -3 to 3
- norm_gain: float32 [256], replicated, may hold values from 0.1 to 1.9
- norm_bias: float32 [256], replicated, may hold values from -3 to 3
- w_in: bfloat16 [256, 1024], replicated, may hold values from -0.375 to 0.375
- b_in: float32 [1024], replicated, may hold values from -3 to 3
- w_out: bfloat16 [1024, 256], replicated, may hold values from -0.1875 to 0.1875
- b_out: float32 [256], replicated, may hold values from -3 to 3
- layer_scale: float32 [256], replicated, may hold values from 0.1 to 1.9
- cotangent: bfloat16 [4, 32, 270, 256], P(('group', 'draw'), 'tile'), parts along dimension 0, may hold values from -6 to 6
Outputs:
- output: bfloat16 [4, 32, 270, 256], P(('group', 'draw'), 'tile'), parts along dimension 0
- input_grad: bfloat16 [4, 32, 270, 256], P(('group', 'draw'), 'tile'), parts along dimension 0
- kernel_grad: float32 [14, 7, 256], P('group'), parts along dimension 0
- w_in_grad: float32 [512, 1024], P('group'), parts along dimension 0
- w_out_grad: float32 [2048, 256], P('group'), parts along dimension 0
- b_in_grad: float32 [2048], P('group'), parts along dimension 0
- channel_grads: float32 [10, 256], P('group'), parts along dimension 0
There are 2 independent parts, one for each index of `group`. A program takes and returns all parts, laid end to end along the dimension named above; an argument that names none is the same for every part. Nothing has to cross between parts.
All inputs are finite; a program needn't handle non-finite values. No bound on the sum of `land_mask` on one device may be relied on, other than what follows from the above.
Results may differ from a plain program's by a relative error of at most 0.007.
Values may be sent and summed in bfloat16 or wider, within the bound.
A program may use at most 64 MiB of HBM per device.

v0:
```python
import functools

import jax
import jax.numpy as jnp
from jax import lax
from jax.experimental import pallas as pl
from jax.experimental.pallas import tpu as pltpu
from jax.sharding import PartitionSpec as P

ROOT_TERM = 0.7978845608028654
CUBIC = 0.044715
EPSILON = 1e-06
F32 = jnp.float32
BF16 = jnp.bfloat16


def block_kernel(
    n,
    scale,
    x_ref,
    cot_ref,
    mask_ref,
    taps_ref,
    conv_bias_ref,
    gain_ref,
    nbias_ref,
    w_in_ref,
    b_in_ref,
    w_out_ref,
    b_out_ref,
    ls_ref,
    out_ref,
    igrad_ref,
    wi_ref,
    wo_ref,
    kgrad_ref,
    bgrad_ref,
    chan_ref,
    xo,
    x_top,
    x_bot,
    cot,
    wrap,
    xs,
    acc,
    hid,
    gact,
    act,
    gh,
    normed,
    gmix,
    gb,
    g_top,
    g_bot,
    gf,
    bsum,
    chan,
    part,
    r1,
    r2,
    r3,
    whole,
    sm,
    s1,
    s2,
    s3,
    s5,
    s6,
    halo_send,
    halo_recv,
    send_sem,
    recv_sem,
    z_send,
    z_recv,
):
    H, W, C = x_ref.shape
    Wp = xo.shape[1]
    B = Wp // 8
    HID = w_in_ref.shape[1]
    m = n // 2
    g = lax.axis_index("group")
    t = lax.axis_index("tile")
    d = lax.axis_index("draw")
    zz = t // 2
    yy = lax.rem(t, 2)
    ty = t + 1 - 2 * yy
    core = (g, t, 1 - d)
    beside = (g, ty, d)
    up = (g, lax.rem(t + n - 1, n), d)
    down = (g, lax.rem(t + 1, n), d)
    zpeer = [(g, 2 * lax.rem(zz + k, m) + yy, d) for k in range(m)]

    def remote(src, dst, ss, rs, dev):
        return pltpu.make_async_remote_copy(
            src_ref=src,
            dst_ref=dst,
            send_sem=ss,
            recv_sem=rs,
            device_id=dev,
            device_id_type=pl.DeviceIdType.MESH,
        )

    barrier = pltpu.get_barrier_semaphore()
    for dev in [core, up, down] + zpeer[1:]:
        pl.semaphore_signal(barrier, inc=1, device_id=dev, device_id_type=pl.DeviceIdType.MESH)
    for p in range(H):
        xo[p, 0:W] = x_ref[p]
        xo[p, W:Wp] = jnp.zeros((Wp - W, C), BF16)
    pl.semaphore_wait(barrier, m + 2)

    @pl.when(t == 0)
    def _():
        x_top[...] = jnp.zeros_like(x_top)
        g_top[...] = jnp.zeros_like(g_top)

    @pl.when(t == n - 1)
    def _():
        x_bot[...] = jnp.zeros_like(x_bot)
        g_bot[...] = jnp.zeros_like(g_bot)

    def to_up(own, bot, a, at):
        k = at + a
        return remote(own.at[a], bot.at[a], halo_send.at[k], halo_recv.at[k], up)

    def to_down(own, top, a, at):
        k = at + 3 + a
        return remote(own.at[H - 3 + a], top.at[a], halo_send.at[k], halo_recv.at[k], down)

    def halo_start(own, top, bot, at, ups, downs):
        @pl.when(t > 0)
        def _():
            for a in ups:
                to_up(own, bot, a, at).start()

        @pl.when(t < n - 1)
        def _():
            for a in downs:
                to_down(own, top, a, at).start()

    def halo_arrive(own, top, bot, at, ups, downs):
        @pl.when(t > 0)
        def _():
            for a in downs:
                to_down(own, top, a, at).wait_recv()

        @pl.when(t < n - 1)
        def _():
            for a in ups:
                to_up(own, bot, a, at).wait_recv()

    def halo_sent(own, top, bot, at):
        @pl.when(t > 0)
        def _():
            for a in range(3):
                to_up(own, bot, a, at).wait_send()

        @pl.when(t < n - 1)
        def _():
            for a in range(3):
                to_down(own, top, a, at).wait_send()

    x_side = (xo, x_top, x_bot, 0)
    g_side = (gb, g_top, g_bot, 6)
    for a in range(3):
        halo_start(*x_side, [a], [2 - a])

    def spread(value, dst, row):
        v = value.astype(F32)
        wrap[8 : 8 + Wp] = v
        wrap[5:8] = v[W - 3 : W]
        wrap[8 + W : 16 + W] = v[0:8]
        for j in range(7):
            dst[j, row] = wrap[5 + j : 5 + j + Wp].reshape(B, 8, C)

    def own_spread(own, dst):
        @pl.loop(0, H)
        def _(r):
            spread(own[r], dst, r + 3)

    def halo_spread(top, bot, dst, ups, downs):
        for a in downs:
            spread(top[a], dst, a)
        for a in ups:
            spread(bot[a], dst, a + H + 3)

    def conv(src, rows, flip, first):
        @pl.loop(0, B // 2)
        def _(c):
            q = pl.ds(c * 2, 2)
            live = [p for p in range(H) if any(0 <= r - p < 7 for r in rows)]
            sums = [acc[p, q] if p in live and not first else None for p in range(H)]
            for j in range(7):
                for r in rows:
                    cells = src[j, r, q]
                    for p in range(H):
                        i = r - p
                        if 0 <= i < 7:
                            tap = (6 - i) * 7 + 6 - j if flip else i * 7 + j
                            term = cells * taps_ref[tap][None]
                            sums[p] = term if sums[p] is None else sums[p] + term
            for p in live:
                acc[p, q] = sums[p]

    own_rows = list(range(3, H + 3))
    own_spread(xo, xs)
    conv(xs, own_rows, False, True)
    for p in range(H):
        cot[p, 0:W] = cot_ref[p].astype(F32)
        cot[p, W:Wp] = jnp.zeros((Wp - W, C), F32)
    bsum[...] = jnp.zeros_like(bsum)
    chan[...] = jnp.zeros_like(chan)
    for a in range(2):
        halo_arrive(*x_side, [a], [2 - a])
        halo_spread(x_top, x_bot, xs, [a], [2 - a])
    conv(xs, [1, 2, H + 3, H + 4], False, False)

    def rowsum(v):
        return jnp.sum(v, axis=0, keepdims=True)

    def pointwise(p):
        conv_out = acc[p].reshape(Wp, C) + conv_bias_ref[...]
        dev = conv_out - jnp.mean(conv_out, axis=-1, keepdims=True)
        rstd = lax.rsqrt(jnp.mean(dev * dev, axis=-1, keepdims=True) + EPSILON)
        unit = dev * rstd
        gf[p] = unit
        normed[p] = (unit * gain_ref[...] + nbias_ref[...]).astype(BF16)
        hid[...] = jnp.dot(normed[p], w_in_ref[...], preferred_element_type=F32)
        ocean = mask_ref[p].astype(F32)
        grad_mixed = (ocean * ls_ref[...] * cot[p]).astype(BF16)
        gmix[p] = grad_mixed
        gact[...] = lax.dot_general(
            grad_mixed, w_out_ref[...], (((1,), (1,)), ((), ())), preferred_element_type=F32
        )

        @pl.loop(0, Wp // 16)
        def _(c):
            q = pl.ds(pl.multiple_of(c * 16, 16), 16)
            h = hid[q] + b_in_ref[...]
            h2 = h * h
            th = jnp.tanh(ROOT_TERM * (h + CUBIC * h2 * h))
            half = 0.5 * (1.0 + th)
            act[p, q] = (h * half).astype(BF16)
            slope = half + 0.5 * h * (1.0 - th * th) * ROOT_TERM * (1.0 + 3.0 * CUBIC * h2)
            grad_hidden = (gact[q] * slope).astype(BF16)
            gh[p, q] = grad_hidden
            wide = grad_hidden.astype(F32)
            bsum[...] += wide[0:8] + wide[8:16]

        mixed = jnp.dot(act[p], w_out_ref[...], preferred_element_type=F32) + b_out_ref[...]
        out_ref[p] = (xo[p].astype(F32) + ocean * ls_ref[...] * mixed).astype(BF16)[0:W]
        grad_normed = lax.dot_general(
            gh[p], w_in_ref[...], (((1,), (1,)), ((), ())), preferred_element_type=F32
        )
        unit = gf[p]
        scaled = grad_normed * gain_ref[...]
        grad_conv = rstd * (
            scaled
            - jnp.mean(scaled, axis=-1, keepdims=True)
            - unit * jnp.mean(scaled * unit, axis=-1, keepdims=True)
        )
        rounded = grad_conv.astype(BF16)
        gb[p] = rounded
        chan[0:1] += rowsum(rounded.astype(F32))
        chan[1:2] += rowsum(grad_normed * unit)
        chan[2:3] += rowsum(grad_normed)
        chan[3:4] += rowsum(gmix[p].astype(F32))
        chan[4:5] += rowsum(ocean * cot[p] * mixed)

    @pl.loop(1, H - 1)
    def _(p):
        pointwise(p)

    halo_start(*g_side, [1, 2], [1, 0])
    halo_arrive(*x_side, [2], [0])
    halo_spread(x_top, x_bot, xs, [2], [0])
    conv(xs, [0, H + 5], False, False)

    @pl.loop(0, 2)
    def _(k):
        pointwise(k * (H - 1))

    halo_start(*g_side, [0], [2])

    flat = H * Wp
    tiles = part.shape[0] * part.shape[1] * part.shape[2] * part.shape[3]
    T = part.shape[3]
    d_in = lax.dot_general(
        normed[...].reshape(flat, C),
        gh[...].reshape(flat, HID),
        (((0,), (0,)), ((), ())),
        preferred_element_type=F32,
    )
    per = C // 16
    for cb in range(HID // C):
        for rb in range(per):
            k = cb * per + rb
            part[k // (tiles // 2), k // (tiles // 4) % 2, k // T % m, k % T, 0:16] = d_in[
                rb * 16 : rb * 16 + 16, cb * C : cb * C + C
            ].astype(BF16)
    d_out = lax.dot_general(
        gmix[...].reshape(flat, C),
        act[...].reshape(flat, HID),
        (((0,), (0,)), ((), ())),
        preferred_element_type=F32,
    ).T
    for k in range(tiles):
        part[k // (tiles // 2), k // (tiles // 4) % 2, k // T % m, k % T, 16:32] = d_out[
            k * 16 : k * 16 + 16
        ].astype(BF16)

    step1 = remote(part.at[1 - d], r1, send_sem.at[0], recv_sem.at[0], core)
    step1.start()

    for j in range(7):

        def tap_terms(c, sums):
            q = pl.ds(c * 2, 2)
            cells16 = pl.ds(pl.multiple_of(c * 16, 16), 16)
            grads = [gb[p, cells16].astype(F32).reshape(2, 8, C) for p in range(H)]
            sums = list(sums)
            for r in range(H + 6):
                cells = xs[j, r, q]
                for p in range(H):
                    i = r - p
                    if 0 <= i < 7:
                        term = cells * grads[p]
                        sums[i] = sums[i] + (term[0] + term[1])
            return tuple(sums)

        sums = lax.fori_loop(0, B // 2, tap_terms, tuple(jnp.zeros((8, C), F32) for _ in range(7)))
        for i in range(7):
            k = i * 7 + j
            sm[k // 32, k % 32 : k % 32 + 1] = rowsum(sums[i])
    step1.wait()
    r1[...] = (part[d].astype(F32) + r1[...].astype(F32)).astype(BF16)
    step2 = remote(r1.at[1 - yy], r2, send_sem.at[1], recv_sem.at[1], beside)
    step2.start()

    hidden_sum = rowsum(bsum[...])
    for k in range(HID // C):
        sm[1, 17 + k : 18 + k] = hidden_sum[:, k * C : k * C + C]
    sm[1, 21:26] = chan[0:5]
    sm[1, 26:32] = jnp.zeros((6, C), F32)

    small1 = remote(sm.at[1 - d], s1, send_sem.at[4], recv_sem.at[4], core)
    small1.start()

    own_spread(gb, xs)
    conv(xs, own_rows, True, True)

    step2.wait()
    r2[...] = (r1[yy].astype(F32) + r2[...].astype(F32)).astype(BF16)
    step3 = [
        remote(r2.at[lax.rem(zz + k, m)], r3.at[k - 1], z_send.at[k - 1], z_recv.at[k - 1], zpeer[k])
        for k in range(1, m)
    ]
    for copy in step3:
        copy.start()
    small1.wait()
    s2[...] = sm[d] + s1[...]
    small2 = remote(s2, s3, send_sem.at[5], recv_sem.at[5], beside)
    small2.start()

    halo_arrive(*g_side, [1, 2], [1, 0])
    halo_spread(g_top, g_bot, xs, [1, 2], [1, 0])

    for copy in step3:
        copy.wait()
    total = r2[zz].astype(F32)
    for k in range(m - 1):
        total = total + r3[k].astype(F32)
    whole[d, yy, zz] = (total * scale).astype(BF16)
    mine = whole.at[d, yy, zz]
    step4 = [
        remote(mine, mine, z_send.at[m - 2 + k], z_recv.at[m - 2 + k], zpeer[k])
        for k in range(1, m)
    ]
    for copy in step4:
        copy.start()
    small2.wait()
    s5[zz] = s2[...] + s3[...]
    small3 = [
        remote(s5.at[zz], s5.at[zz], z_send.at[2 * m - 3 + k], z_recv.at[2 * m - 3 + k], zpeer[k])
        for k in range(1, m)
    ]
    for copy in small3:
        copy.start()

    conv(xs, [0, 1, H + 4, H + 5], True, False)
    halo_arrive(*g_side, [0], [2])
    halo_spread(g_top, g_bot, xs, [0], [2])
    conv(xs, [2, H + 3], True, False)
    halo_sent(*x_side)
    halo_sent(*g_side)

    for copy in step4:
        copy.wait()
    step5 = remote(
        whole.at[d, yy], whole.at[d, yy], send_sem.at[2], recv_sem.at[2], beside
    )
    step5.start()
    for copy in small3:
        copy.wait()
    small_total = s5[0]
    for k in range(1, m):
        small_total = small_total + s5[k]
    s6[d] = small_total * scale
    small4 = remote(s6.at[d], s6.at[d], send_sem.at[6], recv_sem.at[6], core)
    small4.start()
    for p in range(H):
        igrad_ref[p] = (cot[p] + acc[p].reshape(Wp, C)).astype(BF16)[0:W]
    step5.wait()
    step6 = remote(whole.at[d], whole.at[d], send_sem.at[3], recv_sem.at[3], core)
    step6.start()
    small4.wait()
    rows = s6[...].reshape(64, C)
    for i in range(7):
        kgrad_ref[i] = rows[i * 7 : i * 7 + 7]
    for k in range(HID // C):
        bgrad_ref[0:1, k * C : k * C + C] = rows[49 + k : 50 + k]
    chan_ref[...] = rows[49 + HID // C : 54 + HID // C]
    step6.wait()
    for cb in range(HID // C):
        for rb in range(per):
            k = cb * per + rb
            wi_ref[rb * 16 : rb * 16 + 16, cb * C : cb * C + C] = whole[
                k // (tiles // 2), k // (tiles // 4) % 2, k // T % m, k % T, 0:16
            ].astype(F32)
    for k in range(tiles):
        wo_ref[k * 16 : k * 16 + 16] = whole[
            k // (tiles // 2), k // (tiles // 4) % 2, k // T % m, k % T, 16:32
        ].astype(F32)


def per_device(
    n,
    draws,
    inputs,
    land_mask,
    kernel,
    conv_bias,
    norm_gain,
    norm_bias,
    w_in,
    b_in,
    w_out,
    b_out,
    layer_scale,
    cotangent,
):
    _, H, W, C = inputs.shape
    HID = w_in.shape[1]
    Wp = (W + 15) // 16 * 16
    B = Wp // 8
    m = n // 2
    T = HID // 16 // (2 * n)
    scale = float(1.0 / (draws * H * n * W) ** 0.5)
    ocean = jnp.broadcast_to(
        jnp.pad(land_mask, ((0, 0), (0, Wp - W))).astype(BF16)[:, :, None], (H, Wp, C)
    )
    taps = jnp.broadcast_to(kernel.reshape(49, 1, C), (49, 8, C))
    vm = pl.BlockSpec(memory_space=pltpu.VMEM)
    scratch = [
        ((H, Wp, C), BF16),
        ((3, Wp, C), BF16),
        ((3, Wp, C), BF16),
        ((H, Wp, C), F32),
        ((Wp + 16, C), F32),
        ((7, H + 6, B, 8, C), F32),
        ((H, B, 8, C), F32),
        ((Wp, HID), F32),
        ((Wp, HID), F32),
        ((H, Wp, HID), BF16),
        ((H, Wp, HID), BF16),
        ((H, Wp, C), BF16),
        ((H, Wp, C), BF16),
        ((H, Wp, C), BF16),
        ((3, Wp, C), BF16),
        ((3, Wp, C), BF16),
        ((H, Wp, C), F32),
        ((8, HID), F32),
        ((8, C), F32),
        ((2, 2, m, T, 32, C), BF16),
        ((2, m, T, 32, C), BF16),
        ((m, T, 32, C), BF16),
        ((m - 1, T, 32, C), BF16),
        ((2, 2, m, T, 32, C), BF16),
        ((2, 32, C), F32),
        ((32, C), F32),
        ((32, C), F32),
        ((32, C), F32),
        ((m, 32, C), F32),
        ((2, 32, C), F32),
    ]
    output, input_grad, w_in_grad, w_out_grad, kernel_grad, b_in_grad, channel = pl.pallas_call(
        functools.partial(block_kernel, n, scale),
        out_shape=(
            jax.ShapeDtypeStruct((H, W, C), BF16),
            jax.ShapeDtypeStruct((H, W, C), BF16),
            jax.ShapeDtypeStruct((C, HID), F32),
            jax.ShapeDtypeStruct((HID, C), F32),
            jax.ShapeDtypeStruct((7, 7, C), F32),
            jax.ShapeDtypeStruct((1, HID), F32),
            jax.ShapeDtypeStruct((5, C), F32),
        ),
        in_specs=[vm] * 12,
        out_specs=[vm] * 7,
        scratch_shapes=[pltpu.VMEM(shape, dtype) for shape, dtype in scratch]
        + [
            pltpu.SemaphoreType.DMA((12,)),
            pltpu.SemaphoreType.DMA((12,)),
            pltpu.SemaphoreType.DMA((7,)),
            pltpu.SemaphoreType.DMA((7,)),
            pltpu.SemaphoreType.DMA((3 * (m - 1),)),
            pltpu.SemaphoreType.DMA((3 * (m - 1),)),
        ],
        compiler_params=pltpu.CompilerParams(
            collective_id=0, has_side_effects=True, vmem_limit_bytes=60 * 1024 * 1024
        ),
    )(
        inputs[0],
        cotangent[0],
        ocean,
        taps,
        conv_bias[None],
        norm_gain[None],
        norm_bias[None],
        w_in,
        b_in[None],
        w_out,
        b_out[None],
        layer_scale[None],
    )
    return (
        output[None],
        input_grad[None],
        kernel_grad,
        w_in_grad,
        w_out_grad,
        b_in_grad[0],
        channel,
    )


def solution(mesh):
    field = P(("group", "draw"), "tile", None, None)
    placed = (field, P("tile", None)) + (P(),) * 9 + (field,)
    return jax.shard_map(
        functools.partial(per_device, mesh.shape["tile"], mesh.shape["draw"]),
        mesh=mesh,
        in_specs=placed,
        out_specs=(
            field,
            field,
            P("group", None, None),
            P("group", None),
            P("group", None),
            P("group"),
            P("group", None),
        ),
        check_vma=False,
    )
```

profile of v0, /device:TPU:1, one launch (start us, length us, event | category | flops | bytes accessed | tf_op | source)
XLA Modules:
  0.0 87.1 jit_solution(8591749194519924423)
XLA Ops:
  0.6 0.0 copy-start.7
  0.6 0.7 copy-done.7
  1.3 0.0 copy-start.3
  1.4 0.0 copy-start.4
  1.4 0.9 %broadcast_in_dim.38 = f32[49,256]{1,0:T(8,128)S(1)} reshape(f32[7,7,256]{2,1,0:T(8,128)} %param.14) | data formatting | bytes 100352 | tf_op jit(solution)/shard_map/broadcast_in_dim | solution.py:461
  2.3 0.8 broadcast_in_dim.39.taps_ref
  3.1 1.0 %broadcast_in_dim.37.mask_ref = bf16[4,272,256]{2,1,0:T(8,128)(2,1)} broadcast(bf16[4,272]{1,0:T(4,128)(2,1)S(1)} %pad.5), dimensions={0,1} | broadcast | bytes 559232 | tf_op jit(solution)/shard_map/broadcast_in_dim | solution.py:458
  4.1 0.0 copy-done.3
  4.1 0.0 copy-done.4
  4.1 1.1 %copy_bitcast_fusion = (bf16[4,270,256]{2,1,0:T(8,128)(2,1)}, bf16[4,270,256]{2,1,0:T(8,128)(2,1)}) fusion(bf16[1,4,270,256]{3,1,2,0:T(4,128)(2,1)S(1)} %copy-done.3, bf16[1,4,270,256]{3,1,2,0:T(4,128)(2,1)S(1)} %copy-done.4), kind=kLoop, calls=%fused_computation | loop fusion | bytes 2211840 | tf_op jit(solution)/shard_map/squeeze | solution.py:522
  5.2 74.0 %shard_map.171 = (bf16[4,270,256]{2,1,0:T(8,128)(2,1)}, bf16[4,270,256]{2,1,0:T(8,128)(2,1)}, f32[256,1024]{1,0:T(8,128)}, f32[1024,256]{1,0:T(8,128)}, f32[7,7,...) custom-call(bf16[4,270,256]{2,1,0:T(8,128)(2,1)} %get-tuple-element.29.x_ref, ...), custom_call_target="tpu_custom_call" | custom-call | tf_op jit(solution)/shard_map/pallas_call | solution.py:495
  79.2 0.0 copy-start.2
  79.2 0.0 copy-start.1
  79.2 2.3 %copy.21 = bf16[1,4,270,256]{3,1,2,0:T(4,128)(2,1)} copy(bf16[1,4,270,256]{3,2,1,0:T(8,128)(2,1)} %bitcast.14) | data formatting | bytes 1105920
  81.5 0.0 copy-done.2
  81.5 0.0 copy-start.5
  81.5 1.1 %copy.22 = bf16[1,4,270,256]{3,1,2,0:T(4,128)(2,1)} copy(bf16[1,4,270,256]{3,2,1,0:T(8,128)(2,1)S(1)} %bitcast.13) | data formatting | bytes 1105920
  82.6 0.0 copy-done.5
  82.6 0.6 copy.30
  83.2 0.0 copy-done.1
  83.2 0.0 copy-start
  83.2 1.0 %copy.31 = f32[256,1024]{1,0:T(8,128)} copy(f32[256,1024]{1,0:T(8,128)S(1)} %copy-done.1) | data formatting | bytes 2097152
  84.2 0.6 copy-done
  84.8 0.0 copy-start.8
  84.8 1.0 %copy.32 = f32[1024,256]{1,0:T(8,128)} copy(f32[1024,256]{1,0:T(8,128)S(1)} %copy-done) | data formatting | bytes 2097152
  85.8 0.0 copy-done.8
  85.8 0.0 copy-start.6
  85.8 0.6 copy.33
  86.4 0.1 copy-done.6
  86.5 0.6 copy.34
  (2 shorter events, 0.0 us)
Async XLA Ops:
  0.6 0.7 copy-start.7
  1.3 2.7 %copy-start.3 = (bf16[1,4,270,256]{3,1,2,0:T(4,128)(2,1)S(1)}, bf16[1,4,270,256]{3,1,2,0:T(4,128)(2,1)}, u32[]{:S(2)}) copy-start(bf16[1,4,270,256]{3,1,2,0:T(4,128)(2,1)} %param.23) | copy-start | bytes 1658884
  1.4 2.7 %copy-start.4 = (bf16[1,4,270,256]{3,1,2,0:T(4,128)(2,1)S(1)}, bf16[1,4,270,256]{3,1,2,0:T(4,128)(2,1)}, u32[]{:S(2)}) copy-start(bf16[1,4,270,256]{3,1,2,0:T(4,128)(2,1)} %param.12) | copy-start | bytes 1658884
  79.2 2.3 %copy-start.2 = (bf16[4,270,256]{2,1,0:T(8,128)(2,1)S(1)}, bf16[4,270,256]{2,1,0:T(8,128)(2,1)}, u32[]{:S(2)}) copy-start(bf16[4,270,256]{2,1,0:T(8,128)(2,1)} %get-tuple-element.15) | copy-start | bytes 1658884
  79.2 4.0 %copy-start.1 = (f32[256,1024]{1,0:T(8,128)S(1)}, f32[256,1024]{1,0:T(8,128)}, u32[]{:S(2)}) copy-start(f32[256,1024]{1,0:T(8,128)} %get-tuple-element.40) | copy-start | bytes 3145732
  81.5 1.1 %copy-start.5 = (f32[7,7,256]{2,1,0:T(8,128)S(1)}, f32[7,7,256]{2,1,0:T(8,128)}, u32[]{:S(2)}) copy-start(f32[7,7,256]{2,1,0:T(8,128)} %get-tuple-element.39) | copy-start | bytes 150532
  83.2 1.6 %copy-start = (f32[1024,256]{1,0:T(8,128)S(1)}, f32[1024,256]{1,0:T(8,128)}, u32[]{:S(2)}) copy-start(f32[1024,256]{1,0:T(8,128)} %get-tuple-element.41) | copy-start | bytes 3145732
  84.8 1.0 %copy-start.8 = (f32[1,1024]{1,0:T(1,128)S(1)}, f32[1,1024]{1,0:T(1,128)}, u32[]{:S(2)}) copy-start(f32[1,1024]{1,0:T(1,128)} %get-tuple-element.19) | copy-start | bytes 12292
  85.8 0.7 copy-start.6
where the time goes:
time: 87.5 us; the launch traced here: 87.1 us
  Pallas kernels  74 us (85%)
  local copies, waits for them, and re-layouts  12.4 us (14%)
    pallas_call x1, Pallas kernels, per_device(): pl.pallas_call(functools.partial(block_kernel, n, scale), out_shape=(jax....  74 us
    unnamed x25, local copies, waits for them, and re-layouts  8.55 us

commit v1 on v0

v1 whole, which is shorter than its diff:
```python
import functools

import jax
import jax.numpy as jnp
from jax import lax
from jax.experimental import pallas as pl
from jax.experimental.pallas import tpu as pltpu
from jax.sharding import PartitionSpec as P

ROOT_TERM = 0.7978845608028654
CUBIC = 0.044715
EPSILON = 1e-06
F32 = jnp.float32
BF16 = jnp.bfloat16


def block_kernel(
    n,
    scale,
    x_ref,
    cot_ref,
    mask_ref,
    kern_ref,
    conv_bias_ref,
    gain_ref,
    nbias_ref,
    w_in_hbm,
    b_in_ref,
    w_out_hbm,
    b_out_ref,
    ls_ref,
    out_ref,
    igrad_ref,
    wi_ref,
    wo_ref,
    rows_ref,
    xo,
    x_top,
    x_bot,
    cotb,
    mbuf,
    mpad,
    ocean_v,
    taps,
    w_in_ref,
    w_out_ref,
    cot,
    wrap,
    xs,
    acc,
    hid,
    slope_v,
    act,
    gh,
    normed,
    gmix,
    gb,
    g_top,
    g_bot,
    gf,
    rstd_v,
    mixed_v,
    out_v,
    igrad_v,
    bsum,
    chan,
    part,
    r1,
    r2,
    r3,
    whole,
    sm,
    s1,
    s2,
    s3,
    s5,
    s6,
    in_send,
    in_recv,
    in_local,
    back_send,
    back_recv,
    back_local,
    w_local,
    halo_send,
    halo_recv,
    send_sem,
    recv_sem,
    z_send,
    z_recv,
):
    H, W, C = x_ref.shape
    Wp = gb.shape[1]
    B = Wp // 8
    HID = w_in_ref.shape[1]
    m = n // 2
    g = lax.axis_index("group")
    t = lax.axis_index("tile")
    d = lax.axis_index("draw")
    zz = t // 2
    yy = lax.rem(t, 2)
    ty = t + 1 - 2 * yy
    core = (g, t, 1 - d)
    beside = (g, ty, d)
    diag = (g, ty, 1 - d)
    home = yy == d
    away = yy != d
    v = 2 * zz + d

    def at_row(block):
        return (g, 2 * (block // 2) + yy, lax.rem(block, 2))

    up = at_row(lax.rem(v + n - 1, n))
    down = at_row(lax.rem(v + 1, n))
    zpeer = [(g, 2 * lax.rem(zz + k, m) + yy, d) for k in range(m)]

    def remote(src, dst, ss, rs, dev):
        return pltpu.make_async_remote_copy(
            src_ref=src,
            dst_ref=dst,
            send_sem=ss,
            recv_sem=rs,
            device_id=dev,
            device_id_type=pl.DeviceIdType.MESH,
        )

    def moved(src, dst, k):
        return remote(src, dst, in_send.at[k], in_recv.at[k], diag)

    def kept(src, dst, k):
        return pltpu.make_async_copy(src, dst, in_local.at[k])

    load_w = [
        pltpu.make_async_copy(w_in_hbm, w_in_ref, w_local.at[0]),
        pltpu.make_async_copy(w_out_hbm, w_out_ref, w_local.at[1]),
    ]

    @pl.when(home)
    def _():
        for p in range(H):
            kept(x_ref.at[p], xo.at[p], p).start()
        kept(mask_ref, mbuf, 2 * H).start()

    for copy in load_w:
        copy.start()
    barrier = pltpu.get_barrier_semaphore()
    for dev in [core, beside, diag, up, down] + zpeer[1:]:
        pl.semaphore_signal(barrier, inc=1, device_id=dev, device_id_type=pl.DeviceIdType.MESH)
    pl.semaphore_wait(barrier, m + 4)

    def nth(k, end):
        return k + end * (H - 1 - 2 * k)

    @pl.when(away)
    def _():
        for k in range(H):
            p = nth(k, yy)
            moved(x_ref.at[p], xo.at[p], p).start()
        moved(mask_ref, mbuf, 2 * H).start()

    @pl.when(home)
    def _():
        for p in range(H):
            kept(cot_ref.at[p], cotb.at[p], H + p).start()

    for k in range(49):
        taps[k] = jnp.broadcast_to(kern_ref[k // 7, k % 7 : k % 7 + 1, :], (8, C))

    @pl.when(v == 0)
    def _():
        x_top[...] = jnp.zeros_like(x_top)
        g_top[...] = jnp.zeros_like(g_top)

    @pl.when(v == n - 1)
    def _():
        x_bot[...] = jnp.zeros_like(x_bot)
        g_bot[...] = jnp.zeros_like(g_bot)

    def to_up(own, bot, a, at):
        k = at + a
        return remote(own.at[a], bot.at[a], halo_send.at[k], halo_recv.at[k], up)

    def to_down(own, top, a, at):
        k = at + 3 + a
        return remote(own.at[a + H - 3], top.at[a], halo_send.at[k], halo_recv.at[k], down)

    def row_ready(own, top, bot, at, q):
        @pl.when(jnp.logical_and(v > 0, q < 3))
        def _():
            to_up(own, bot, q, at).start()

        @pl.when(jnp.logical_and(v < n - 1, q >= H - 3))
        def _():
            to_down(own, top, q - (H - 3), at).start()

    def halo_arrive(own, top, bot, at, ups, downs):
        @pl.when(v > 0)
        def _():
            for a in downs:
                to_down(own, top, a, at).wait_recv()

        @pl.when(v < n - 1)
        def _():
            for a in ups:
                to_up(own, bot, a, at).wait_recv()

    def halo_sent(own, top, bot, at):
        @pl.when(v > 0)
        def _():
            for a in range(3):
                to_up(own, bot, a, at).wait_send()

        @pl.when(v < n - 1)
        def _():
            for a in range(3):
                to_down(own, top, a, at).wait_send()

    x_side = (xo, x_top, x_bot, 0)
    g_side = (gb, g_top, g_bot, 6)

    def spread(value, dst, row):
        rows = value.shape[0]
        wrap[8 : 8 + rows] = value.astype(F32)
        wrap[5:8] = wrap[5 + W : 8 + W]
        wrap[8 + W : 16 + W] = wrap[8:16]
        for j in range(7):
            dst[j, row] = wrap[5 + j : 5 + j + Wp].reshape(B, 8, C)

    def halo_spread(top, bot, dst, ups, downs):
        for a in downs:
            spread(top[a], dst, a)
        for a in ups:
            spread(bot[a], dst, a + H + 3)

    def conv(src, rows, flip, first, outs=tuple(range(4))):
        @pl.loop(0, B // 2)
        def _(c):
            q = pl.ds(c * 2, 2)
            live = [p for p in outs if any(0 <= r - p < 7 for r in rows)]
            sums = [acc[p, q] if p in live and not first else None for p in range(H)]
            for j in range(7):
                for r in rows:
                    cells = src[j, r, q]
                    for p in live:
                        i = r - p
                        if 0 <= i < 7:
                            tap = (6 - i) * 7 + 6 - j if flip else i * 7 + j
                            term = cells * taps[tap][None]
                            sums[p] = term if sums[p] is None else sums[p] + term
            for p in live:
                acc[p, q] = sums[p]

    own_rows = list(range(3, H + 3))

    @pl.loop(0, H)
    def _(k):
        q = nth(k, d)

        @pl.when(home)
        def _():
            kept(x_ref.at[q], xo.at[q], q).wait()

        @pl.when(away)
        def _():
            moved(x_ref.at[q], xo.at[q], q).wait_recv()

        row_ready(*x_side, q)
        spread(xo[q], xs, q + 3)

    @pl.when(away)
    def _():
        for p in range(H):
            moved(x_ref.at[p], xo.at[p], p).wait_send()
        for p in range(H):
            moved(cot_ref.at[p], cotb.at[p], H + p).start()

    conv(xs, own_rows, False, True)

    @pl.when(home)
    def _():
        kept(mask_ref, mbuf, 2 * H).wait()

    @pl.when(away)
    def _():
        moved(mask_ref, mbuf, 2 * H).wait()

    mpad[...] = jnp.zeros_like(mpad)
    mpad[0:H, 0:W] = mbuf[...].astype(F32)
    flags = mpad[...].astype(BF16)
    lines = lax.broadcasted_iota(jnp.int32, (mpad.shape[0], C), 0)
    for p in range(H):
        pick = jnp.where(lines == p, 1.0, 0.0).astype(BF16)
        ocean_v[p] = lax.dot_general(
            flags, pick, (((0,), (0,)), ((), ())), preferred_element_type=F32
        ).astype(BF16)
    bsum[...] = jnp.zeros_like(bsum)
    chan[...] = jnp.zeros_like(chan)
    for copy in load_w:
        copy.wait()
    halo_arrive(*x_side, [0, 1, 2], [0, 1, 2])
    halo_spread(x_top, x_bot, xs, [0, 1, 2], [0, 1, 2])
    conv(xs, [0, 1, 2, H + 3, H + 4, H + 5], False, False)

    def rowsum(value):
        return jnp.sum(value, axis=0, keepdims=True)

    def give_back(src, dst, k):
        return remote(src, dst, back_send.at[k], back_recv.at[k], diag)

    def put(src, dst, k):
        return pltpu.make_async_copy(src, dst, back_local.at[k])

    def returned(src, dst, k):
        @pl.when(home)
        def _():
            put(src, dst, k).start()

        @pl.when(away)
        def _():
            give_back(src, dst, k).start()

    @pl.loop(0, H)
    def _(p):
        conv_out = acc[p].reshape(Wp, C) + conv_bias_ref[...]
        dev = conv_out - jnp.mean(conv_out, axis=-1, keepdims=True)
        rstd = lax.rsqrt(jnp.mean(dev * dev, axis=-1, keepdims=True) + EPSILON)
        unit = dev * rstd
        rstd_v[p] = jnp.broadcast_to(rstd, (Wp, 128))
        gf[p] = unit
        normed[p] = (unit * gain_ref[...] + nbias_ref[...]).astype(BF16)
        hid[...] = jnp.dot(normed[p], w_in_ref[...], preferred_element_type=F32)

        @pl.loop(0, Wp // 16)
        def _(c):
            q = pl.ds(pl.multiple_of(c * 16, 16), 16)
            h = hid[q] + b_in_ref[...]
            h2 = h * h
            th = jnp.tanh(h * (h2 * (ROOT_TERM * CUBIC) + ROOT_TERM))
            half = 0.5 * th + 0.5
            a = h * half
            act[p, q] = a.astype(BF16)
            slope_v[p, q] = half + (a - a * th) * (h2 * (3.0 * CUBIC * ROOT_TERM) + ROOT_TERM)

        mixed = jnp.dot(act[p], w_out_ref[...], preferred_element_type=F32) + b_out_ref[...]
        mixed_v[p] = mixed
        ocean = ocean_v[p].astype(F32)
        out_v[p] = (xo[p].astype(F32) + (ocean * ls_ref[...] * mixed)[0:W]).astype(BF16)
        returned(out_v.at[p], out_ref.at[p], p)

    @pl.when(home)
    def _():
        for p in range(H):
            kept(cot_ref.at[p], cotb.at[p], H + p).wait()

    @pl.when(away)
    def _():
        for p in range(H):
            moved(cot_ref.at[p], cotb.at[p], H + p).wait()

    @pl.loop(0, H)
    def _(p):
        cot[p, 0:W] = cotb[p].astype(F32)
        cot[p, W:Wp] = jnp.zeros((Wp - W, C), F32)
        masked = ocean_v[p].astype(F32) * cot[p]
        grad_mixed = (ls_ref[...] * masked).astype(BF16)
        gmix[p] = grad_mixed
        chan[3:4] += rowsum(grad_mixed.astype(F32))
        chan[4:5] += rowsum(masked * mixed_v[p])

    flat = H * Wp
    T = part.shape[4]
    tiles = 4 * m * T
    per = C // 16

    class Exchange:
        def __init__(self, w):
            self.w = w
            self.s = 4 * w
            self.z = 2 * (m - 1) * w

        def fill(self, tile):
            for k in range(tiles):
                part[self.w, k // (tiles // 2), k // (tiles // 4) % 2, k // T % m, k % T] = tile(
                    k
                ).astype(BF16)
            self.one().start()

        def one(self):
            w, s = self.w, self.s
            return remote(part.at[w, 1 - d], r1.at[w], send_sem.at[s], recv_sem.at[s], core)

        def two(self):
            w, s = self.w, self.s + 1
            return remote(r1.at[w, 1 - yy], r2.at[w], send_sem.at[s], recv_sem.at[s], beside)

        def three(self):
            w = self.w
            return [
                remote(
                    r2.at[w, lax.rem(zz + k, m)],
                    r3.at[w, k - 1],
                    z_send.at[self.z + k - 1],
                    z_recv.at[self.z + k - 1],
                    zpeer[k],
                )
                for k in range(1, m)
            ]

        def four(self):
            mine = whole.at[self.w, d, yy, zz]
            return [
                remote(
                    mine,
                    mine,
                    z_send.at[self.z + m - 2 + k],
                    z_recv.at[self.z + m - 2 + k],
                    zpeer[k],
                )
                for k in range(1, m)
            ]

        def five(self):
            mine = whole.at[self.w, d, yy]
            s = self.s + 2
            return remote(mine, mine, send_sem.at[s], recv_sem.at[s], beside)

        def six(self):
            mine = whole.at[self.w, d]
            s = self.s + 3
            return remote(mine, mine, send_sem.at[s], recv_sem.at[s], core)

        def after_one(self):
            w = self.w
            self.one().wait()
            r1[w] = (part[w, d].astype(F32) + r1[w].astype(F32)).astype(BF16)
            self.two().start()

        def after_two(self):
            w = self.w
            self.two().wait()
            r2[w] = (r1[w, yy].astype(F32) + r2[w].astype(F32)).astype(BF16)
            for copy in self.three():
                copy.start()

        def after_three(self):
            w = self.w
            for copy in self.three():
                copy.wait()
            total = r2[w, zz].astype(F32)
            for k in range(m - 1):
                total = total + r3[w, k].astype(F32)
            whole[w, d, yy, zz] = (total * scale).astype(BF16)
            for copy in self.four():
                copy.start()

        def after_four(self):
            for copy in self.four():
                copy.wait()
            self.five().start()

        def after_five(self):
            self.five().wait()
            self.six().start()

        def after_six(self):
            self.six().wait()

    ex_out = Exchange(0)
    ex_in = Exchange(1)

    d_out = lax.dot_general(
        gmix[...].reshape(flat, C),
        act[...].reshape(flat, HID),
        (((0,), (0,)), ((), ())),
        preferred_element_type=F32,
    ).T
    ex_out.fill(lambda k: d_out[k * 16 : k * 16 + 16])

    @pl.loop(0, H)
    def _(k):
        p = nth(k, d)
        hid[...] = lax.dot_general(
            gmix[p], w_out_ref[...], (((1,), (1,)), ((), ())), preferred_element_type=F32
        )

        @pl.loop(0, Wp // 16)
        def _(c):
            q = pl.ds(pl.multiple_of(c * 16, 16), 16)
            grad_hidden = (hid[q] * slope_v[p, q]).astype(BF16)
            gh[p, q] = grad_hidden
            wide = grad_hidden.astype(F32)
            bsum[...] += wide[0:8] + wide[8:16]

        grad_normed = lax.dot_general(
            gh[p], w_in_ref[...], (((1,), (1,)), ((), ())), preferred_element_type=F32
        )
        unit = gf[p]
        scaled = grad_normed * gain_ref[...]
        grad_conv = rstd_v[p][:, 0:1] * (
            scaled
            - jnp.mean(scaled, axis=-1, keepdims=True)
            - unit * jnp.mean(scaled * unit, axis=-1, keepdims=True)
        )
        rounded = grad_conv.astype(BF16)
        gb[p] = rounded
        row_ready(*g_side, p)
        chan[0:1] += rowsum(rounded.astype(F32))
        chan[1:2] += rowsum(grad_normed * unit)
        chan[2:3] += rowsum(grad_normed)

        @pl.when(k == 0)
        def _():
            ex_out.after_one()

        @pl.when(k == 2)
        def _():
            ex_out.after_two()

    d_in = lax.dot_general(
        normed[...].reshape(flat, C),
        gh[...].reshape(flat, HID),
        (((0,), (0,)), ((), ())),
        preferred_element_type=F32,
    )
    ex_in.fill(
        lambda k: d_in[k % per * 16 : k % per * 16 + 16, k // per * C : k // per * C + C]
    )
    ex_out.after_three()

    for j in range(7):

        def tap_terms(c, sums):
            q = pl.ds(c * 2, 2)
            cells16 = pl.ds(pl.multiple_of(c * 16, 16), 16)
            grads = [gb[p, cells16].astype(F32).reshape(2, 8, C) for p in range(H)]
            sums = list(sums)
            for r in range(H + 6):
                cells = xs[j, r, q]
                for p in range(H):
                    i = r - p
                    if 0 <= i < 7:
                        term = cells * grads[p]
                        sums[i] = sums[i] + (term[0] + term[1])
            return tuple(sums)

        sums = lax.fori_loop(0, B // 2, tap_terms, tuple(jnp.zeros((8, C), F32) for _ in range(7)))
        for i in range(7):
            k = i * 7 + j
            sm[k // 32, k % 32 : k % 32 + 1] = rowsum(sums[i])
        if j == 1:
            ex_in.after_one()
        if j == 4:
            ex_in.after_two()
            ex_out.after_four()

    hidden_sum = rowsum(bsum[...])
    for k in range(HID // C):
        sm[1, 17 + k : 18 + k] = hidden_sum[:, k * C : k * C + C]
    sm[1, 21:26] = chan[0:5]
    sm[1, 26:32] = jnp.zeros((6, C), F32)

    small1 = remote(sm.at[1 - d], s1, send_sem.at[8], recv_sem.at[8], core)
    small1.start()

    @pl.loop(0, H)
    def _(r):
        spread(gb[r], xs, r + 3)

    ex_in.after_three()
    small1.wait()
    s2[...] = sm[d] + s1[...]
    small2 = remote(s2, s3, send_sem.at[9], recv_sem.at[9], beside)
    small2.start()
    ex_out.after_five()

    halo_arrive(*g_side, [0, 1, 2], [0, 1, 2])
    halo_spread(g_top, g_bot, xs, [0, 1, 2], [0, 1, 2])
    near, far = (0, 1), (2, 3)

    def finish(rows):
        for p in rows:
            igrad_v[p] = (cot[p] + acc[p].reshape(Wp, C)).astype(BF16)[0:W]
            returned(igrad_v.at[p], igrad_ref.at[p], H + p)

    conv(xs, list(range(0, 8)), True, True, near)
    finish(near)
    ex_in.after_four()
    small2.wait()
    s5[zz] = s2[...] + s3[...]
    zs = 4 * (m - 1) - 1
    small3 = [
        remote(s5.at[zz], s5.at[zz], z_send.at[zs + k], z_recv.at[zs + k], zpeer[k])
        for k in range(1, m)
    ]
    for copy in small3:
        copy.start()
    conv(xs, list(range(2, 10)), True, True, far)
    finish(far)
    ex_in.after_five()
    for copy in small3:
        copy.wait()
    small_total = s5[0]
    for k in range(1, m):
        small_total = small_total + s5[k]
    s6[d] = small_total * scale
    small4 = remote(s6.at[d], s6.at[d], send_sem.at[10], recv_sem.at[10], core)
    small4.start()
    halo_sent(*x_side)
    halo_sent(*g_side)
    ex_out.after_six()
    last = [pltpu.make_async_copy(whole.at[0], wo_ref, w_local.at[0])]
    last[0].start()
    small4.wait()
    last.append(pltpu.make_async_copy(s6, rows_ref, w_local.at[2]))
    last[1].start()
    ex_in.after_six()
    last.append(pltpu.make_async_copy(whole.at[1], wi_ref, w_local.at[1]))
    last[2].start()
    for k in range(2 * H):
        src, dst = ((out_v, out_ref), (igrad_v, igrad_ref))[k // H]

        @pl.when(home)
        def _():
            put(src.at[k % H], dst.at[k % H], k).wait()

        @pl.when(away)
        def _():
            give_back(src.at[k % H], dst.at[k % H], k).wait()

    for copy in last:
        copy.wait()


def gather_kernel(wi_part, wo_part, rows_part, wi_ref, wo_ref, kgrad_ref, bgrad_ref, chan_ref):
    C = wi_ref.shape[0]
    HID = wi_ref.shape[1]
    per = C // 16
    _, _, m, T, _, _ = wi_part.shape
    tiles = 4 * m * T
    rows = rows_part[...].reshape(64, C)
    for i in range(7):
        kgrad_ref[i] = rows[i * 7 : i * 7 + 7]
    for k in range(HID // C):
        bgrad_ref[0:1, k * C : k * C + C] = rows[49 + k : 50 + k]
    chan_ref[...] = rows[49 + HID // C : 54 + HID // C]
    for k in range(tiles):
        at = (k // (tiles // 2), k // (tiles // 4) % 2, k // T % m, k % T)
        rb, cb = k % per, k // per
        wi_ref[rb * 16 : rb * 16 + 16, cb * C : cb * C + C] = wi_part[at].astype(F32)
        wo_ref[k * 16 : k * 16 + 16] = wo_part[at].astype(F32)


def per_device(
    n,
    draws,
    inputs,
    land_mask,
    kernel,
    conv_bias,
    norm_gain,
    norm_bias,
    w_in,
    b_in,
    w_out,
    b_out,
    layer_scale,
    cotangent,
):
    _, H, W, C = inputs.shape
    HID = w_in.shape[1]
    Wp = (W + 15) // 16 * 16
    B = Wp // 8
    m = n // 2
    T = HID // 16 // (2 * n)
    scale = float(1.0 / (draws * H * n * W) ** 0.5)
    vm = pl.BlockSpec(memory_space=pltpu.VMEM)
    hbm = pl.BlockSpec(memory_space=pl.ANY)
    scratch = [
        ((H, W, C), BF16),
        ((3, W, C), BF16),
        ((3, W, C), BF16),
        ((H, W, C), BF16),
        ((H, W), jnp.int32),
        ((16, Wp), F32),
        ((H, Wp, C), BF16),
        ((49, 8, C), F32),
        ((C, HID), BF16),
        ((HID, C), BF16),
        ((H, Wp, C), F32),
        ((Wp + 16, C), F32),
        ((7, H + 6, B, 8, C), F32),
        ((H, B, 8, C), F32),
        ((Wp, HID), F32),
        ((H, Wp, HID), F32),
        ((H, Wp, HID), BF16),
        ((H, Wp, HID), BF16),
        ((H, Wp, C), BF16),
        ((H, Wp, C), BF16),
        ((H, Wp, C), BF16),
        ((3, Wp, C), BF16),
        ((3, Wp, C), BF16),
        ((H, Wp, C), F32),
        ((H, Wp, 128), F32),
        ((H, Wp, C), F32),
        ((H, W, C), BF16),
        ((H, W, C), BF16),
        ((8, HID), F32),
        ((8, C), F32),
        ((2, 2, 2, m, T, 16, C), BF16),
        ((2, 2, m, T, 16, C), BF16),
        ((2, m, T, 16, C), BF16),
        ((2, m - 1, T, 16, C), BF16),
        ((2, 2, 2, m, T, 16, C), BF16),
        ((2, 32, C), F32),
        ((32, C), F32),
        ((32, C), F32),
        ((32, C), F32),
        ((m, 32, C), F32),
        ((2, 32, C), F32),
    ]
    dma = pltpu.SemaphoreType.DMA
    output, input_grad, wi_part, wo_part, rows_part = pl.pallas_call(
        functools.partial(block_kernel, n, scale),
        out_shape=(
            jax.ShapeDtypeStruct((H, W, C), BF16),
            jax.ShapeDtypeStruct((H, W, C), BF16),
            jax.ShapeDtypeStruct((2, 2, m, T, 16, C), BF16),
            jax.ShapeDtypeStruct((2, 2, m, T, 16, C), BF16),
            jax.ShapeDtypeStruct((2, 32, C), F32),
        ),
        in_specs=[hbm, hbm, hbm, vm, vm, vm, vm, hbm, vm, hbm, vm, vm],
        out_specs=[hbm] * 5,
        scratch_shapes=[pltpu.VMEM(shape, dtype) for shape, dtype in scratch]
        + [
            dma((2 * H + 1,)),
            dma((2 * H + 1,)),
            dma((2 * H + 1,)),
            dma((2 * H,)),
            dma((2 * H,)),
            dma((2 * H,)),
            dma((3,)),
            dma((12,)),
            dma((12,)),
            dma((11,)),
            dma((11,)),
            dma((5 * (m - 1),)),
            dma((5 * (m - 1),)),
        ],
        compiler_params=pltpu.CompilerParams(
            collective_id=0, has_side_effects=True, vmem_limit_bytes=60 * 1024 * 1024
        ),
        name="block",
    )(
        inputs[0],
        cotangent[0],
        land_mask,
        kernel,
        conv_bias[None],
        norm_gain[None],
        norm_bias[None],
        w_in,
        b_in[None],
        w_out,
        b_out[None],
        layer_scale[None],
    )
    w_in_grad, w_out_grad, kernel_grad, b_in_grad, channel = pl.pallas_call(
        gather_kernel,
        out_shape=(
            jax.ShapeDtypeStruct((C, HID), F32),
            jax.ShapeDtypeStruct((HID, C), F32),
            jax.ShapeDtypeStruct((7, 7, C), F32),
            jax.ShapeDtypeStruct((1, HID), F32),
            jax.ShapeDtypeStruct((5, C), F32),
        ),
        in_specs=[vm] * 3,
        out_specs=[vm] * 5,
        name="gather",
    )(wi_part, wo_part, rows_part)
    return (
        output[None],
        input_grad[None],
        kernel_grad,
        w_in_grad,
        w_out_grad,
        b_in_grad[0],
        channel,
    )


def solution(mesh):
    field = P(("group", "draw"), "tile", None, None)
    placed = (field, P("tile", None)) + (P(),) * 9 + (field,)
    return jax.shard_map(
        functools.partial(per_device, mesh.shape["tile"], mesh.shape["draw"]),
        mesh=mesh,
        in_specs=placed,
        out_specs=(
            field,
            field,
            P("group", None, None),
            P("group", None),
            P("group", None),
            P("group"),
            P("group", None),
        ),
        check_vma=False,
    )
```

time: 87.5 us -> 77.5 us (0.89)
  local copies, waits for them, and re-layouts: 12.4 us -> 5.65 us
  Pallas kernels: 74 us -> 71 us
    pallas_call x1, Pallas kernels: 74 us -> 68.4 us  [per_device(): pl.pallas_call(functools.partial(block_kernel, n, scale), out_shape=(jax....]
    unnamed x25 -> x4, local copies, waits for them, and re-layouts: 8.55 us -> 3.29 us
    broadcast_in_dim x3 -> x0, local copies, waits for them, and re-layouts: 2.72 us -> none  [the longest x2 1.69 us: per_device(): taps = jnp.broadcast_to(kernel.reshape(49, 1, C), (49, 8, C))]
    pallas_call x0 -> x1, Pallas kernels: none -> 2.61 us  [per_device(): pl.pallas_call(gather_kernel, out_shape=(jax.ShapeDtypeStruct((C, HID), F...]
    squeeze x1, local copies, waits for them, and re-layouts: 1.14 us -> 2.35 us  [per_device(): cotangent[0]]
where the time goes in v1:
time: 77.5 us; the launch traced here: 77.3 us
  Pallas kernels  71 us (92%)
  local copies, waits for them, and re-layouts  5.65 us (7%)
    pallas_call x1, Pallas kernels, per_device(): pl.pallas_call(functools.partial(block_kernel, n, scale), out_shape=(jax....  68.4 us
    unnamed x4, local copies, waits for them, and re-layouts  3.29 us
    pallas_call x1, Pallas kernels, per_device(): pl.pallas_call(gather_kernel, out_shape=(jax.ShapeDtypeStruct((C, HID), F...  2.61 us
    squeeze x1, local copies, waits for them, and re-layouts, per_device(): cotangent[0]  2.35 us

profile of v1, /device:TPU:1, one launch (start us, length us, event | category | flops | bytes accessed | tf_op | source)
XLA Modules:
  0.0 77.3 jit_solution(7557239841974099211)
XLA Ops:
  0.6 2.4 %copy_bitcast_fusion = (bf16[4,270,256]{2,1,0:T(8,128)(2,1)}, bf16[4,270,256]{2,1,0:T(8,128)(2,1)}) fusion(bf16[1,4,270,256]{3,1,2,0:T(4,128)(2,1)} %param.23, bf16[1,4,270,256]{3,1,2,0:T(4,128)(2,1)} %param.12), kind=kLoop, calls=%fused_computation | loop fusion | bytes 2211840 | tf_op jit(solution)/shard_map/squeeze | solution.py:755
  3.0 68.4 %block.1 = (bf16[4,270,256]{2,1,0:T(8,128)(2,1)}, bf16[4,270,256]{2,1,0:T(8,128)(2,1)}, bf16[2,2,4,4,16,256]{5,4,3,2,1,0:T(8,128)(2,1)}, bf16[2,2,4,4,16,256]{5,4,3,2,1,0:T(8,128)(2,1)}, f32[2,32,256]{2,1,0:T(8,128)}) custom-call(bf16[4,270,256]{2,1,0:T(8,128)(2,1)} %get-tuple-element.35.x_ref, bf16[4,270,256]{2,1,0:T(8,128)(2,1)} %get-tuple-element.34.cot_ref, ...), custom_call_target="tpu_custom_call" | custom-call | tf_op jit(solution)/shard_map/block/pallas_call | solution.py:722
  71.4 0.0 copy-start
  71.4 2.2 %copy.21 = bf16[1,4,270,256]{3,1,2,0:T(4,128)(2,1)} copy(bf16[1,4,270,256]{3,2,1,0:T(8,128)(2,1)} %bitcast.14) | data formatting | bytes 1105920
  73.6 0.0 copy-done
  73.6 1.1 %copy.22 = bf16[1,4,270,256]{3,1,2,0:T(4,128)(2,1)} copy(bf16[1,4,270,256]{3,2,1,0:T(8,128)(2,1)S(1)} %bitcast.13) | data formatting | bytes 1105920
  74.7 2.6 %gather.1 = (f32[256,1024]{1,0:T(8,128)}, f32[1024,256]{1,0:T(8,128)}, f32[7,7,256]{2,1,0:T(8,128)}, f32[1,1024]{1,0:T(1,128)}, f32[5,256]{1,0:T(8,128)}) custom-call(bf16[2,2,4,4,16,256]{5,4,3,2,1,0:T(8,128)(2,1)} %get-tuple-element.19.wi_part, bf16[2,2,4,4,16,256]{5,4,3,2,1,0:T(8,128)(2,1)} %get-tuple-element.20.wo_part, ...), custom_call_target="tpu_custom_call" | custom-call | tf_op jit(solution)/shard_map/gather/pallas_call | solution.py:767
Async XLA Ops:
  71.4 2.2 %copy-start = (bf16[4,270,256]{2,1,0:T(8,128)(2,1)S(1)}, bf16[4,270,256]{2,1,0:T(8,128)(2,1)}, u32[]{:S(2)}) copy-start(bf16[4,270,256]{2,1,0:T(8,128)(2,1)} %get-tuple-element.18) | copy-start | bytes 1658884

commit v2 on v1

v2 whole, which is shorter than its diff:
```python
import functools

import jax
import jax.numpy as jnp
from jax import lax
from jax.experimental import pallas as pl
from jax.experimental.pallas import tpu as pltpu
from jax.sharding import PartitionSpec as P

ROOT_TERM = 0.7978845608028654
CUBIC = 0.044715
EPSILON = 1e-06
F32 = jnp.float32
BF16 = jnp.bfloat16


def block_kernel(
    n,
    scale,
    x_ref,
    cot_ref,
    mask_ref,
    kern_ref,
    conv_bias_ref,
    gain_ref,
    nbias_ref,
    w_in_hbm,
    b_in_ref,
    w_out_hbm,
    b_out_ref,
    ls_ref,
    out_ref,
    igrad_ref,
    wi_ref,
    wo_ref,
    rows_ref,
    xo,
    x_top,
    x_bot,
    cotb,
    mbuf,
    mpad,
    ocean_v,
    taps,
    w_in_ref,
    w_out_ref,
    wx,
    xs,
    acc,
    hid,
    slope_v,
    act,
    gh,
    normed,
    gmix,
    gb,
    g_top,
    g_bot,
    gf,
    rstd_v,
    mixed_v,
    out_v,
    igrad_v,
    bsum,
    chan,
    part,
    r1,
    r2,
    r3,
    whole,
    sm,
    s1,
    s2,
    s3,
    s5,
    s6,
    in_send,
    in_recv,
    in_local,
    back_send,
    back_recv,
    back_local,
    w_local,
    halo_send,
    halo_recv,
    send_sem,
    recv_sem,
    z_send,
    z_recv,
):
    H, Wp, C = x_ref.shape
    W = mbuf.shape[1]
    B = Wp // 8
    HID = w_in_ref.shape[1]
    U = Wp // 16
    ends = [(U * k + 3) // 4 * 16 for k in range(5)]
    chunks = list(zip(ends[:-1], ends[1:]))
    inner = [0] + [e + 16 for e in ends[1:-1]] + [Wp - 16]
    segs = [(Wp - 16, Wp)] + list(zip(inner[:-1], inner[1:]))
    m = n // 2
    g = lax.axis_index("group")
    t = lax.axis_index("tile")
    d = lax.axis_index("draw")
    zz = t // 2
    yy = lax.rem(t, 2)
    ty = t + 1 - 2 * yy
    core = (g, t, 1 - d)
    beside = (g, ty, d)
    diag = (g, ty, 1 - d)
    home = yy == d
    away = yy != d
    v = 2 * zz + d

    def at_row(block):
        return (g, 2 * (block // 2) + yy, lax.rem(block, 2))

    up = at_row(lax.rem(v + n - 1, n))
    down = at_row(lax.rem(v + 1, n))
    zpeer = [(g, 2 * lax.rem(zz + k, m) + yy, d) for k in range(m)]

    def remote(src, dst, ss, rs, dev):
        return pltpu.make_async_remote_copy(
            src_ref=src,
            dst_ref=dst,
            send_sem=ss,
            recv_sem=rs,
            device_id=dev,
            device_id_type=pl.DeviceIdType.MESH,
        )

    def moved(src, dst, k):
        return remote(src, dst, in_send.at[k], in_recv.at[k], diag)

    def kept(src, dst, k):
        return pltpu.make_async_copy(src, dst, in_local.at[k])

    load_w = [
        pltpu.make_async_copy(w_in_hbm, w_in_ref, w_local.at[0]),
        pltpu.make_async_copy(w_out_hbm, w_out_ref, w_local.at[1]),
    ]

    def seg(ref, k):
        lo, hi = segs[k]
        return ref.at[:, lo:hi]

    def chunk(ref, k):
        lo, hi = chunks[k]
        return ref.at[:, lo:hi]

    N = len(segs)
    K = len(chunks)

    def x_args(k):
        return seg(x_ref, k), seg(xo, k), k

    def cot_args(k):
        return chunk(cot_ref, k), chunk(cotb, k), N + k

    mask_args = (mask_ref, mbuf, N + K)

    @pl.when(home)
    def _():
        for k in range(N):
            kept(*x_args(k)).start()
        kept(*mask_args).start()

    for copy in load_w:
        copy.start()
    barrier = pltpu.get_barrier_semaphore()
    for dev in [core, beside, diag, up, down] + zpeer[1:]:
        pl.semaphore_signal(barrier, inc=1, device_id=dev, device_id_type=pl.DeviceIdType.MESH)
    pl.semaphore_wait(barrier, m + 4)

    @pl.when(away)
    def _():
        for k in range(N):
            moved(*x_args(k)).start()
        moved(*mask_args).start()

    @pl.when(home)
    def _():
        for k in range(K):
            kept(*cot_args(k)).start()

    for k in range(49):
        taps[k] = jnp.broadcast_to(kern_ref[k // 7, k % 7 : k % 7 + 1, :], (8, C))

    @pl.when(v == 0)
    def _():
        x_top[...] = jnp.zeros_like(x_top)
        g_top[...] = jnp.zeros_like(g_top)

    @pl.when(v == n - 1)
    def _():
        x_bot[...] = jnp.zeros_like(x_bot)
        g_bot[...] = jnp.zeros_like(g_bot)

    def to_up(own, bot, span, k):
        lo, hi = span
        return remote(
            own.at[0:3, lo:hi], bot.at[:, lo:hi], halo_send.at[2 * k], halo_recv.at[2 * k], up
        )

    def to_down(own, top, span, k):
        lo, hi = span
        k = 2 * k + 1
        return remote(
            own.at[H - 3 : H, lo:hi], top.at[:, lo:hi], halo_send.at[k], halo_recv.at[k], down
        )

    def halo_start(own, top, bot, span, k):
        @pl.when(v > 0)
        def _():
            to_up(own, bot, span, k).start()

        @pl.when(v < n - 1)
        def _():
            to_down(own, top, span, k).start()

    def halo_arrive(own, top, bot, span, k):
        @pl.when(v > 0)
        def _():
            to_down(own, top, span, k).wait_recv()

        @pl.when(v < n - 1)
        def _():
            to_up(own, bot, span, k).wait_recv()

    def halo_sent(own, top, bot, span, k):
        @pl.when(v > 0)
        def _():
            to_up(own, bot, span, k).wait_send()

        @pl.when(v < n - 1)
        def _():
            to_down(own, top, span, k).wait_send()

    x_side = (xo, x_top, x_bot)
    g_side = (gb, g_top, g_bot)

    def widen(value, first, lo):
        rows, size, _ = value.shape
        wx[first : first + rows, 8 + lo : 8 + lo + size] = value.astype(F32)

    def spread(span):
        lo, hi = span

        @pl.loop(0, H + 6)
        def _(r):
            for j in range(7):
                xs[j, r, lo // 8 : hi // 8] = wx[r, 5 + j + lo : 5 + j + hi].reshape(
                    (hi - lo) // 8, 8, C
                )

    def wrap_left():
        wx[:, 5:8] = wx[:, 5 + W : 8 + W]

    def wrap_right():
        wx[:, 8 + W : 16 + W] = wx[:, 8:16]

    def conv(span, flip):
        for j in range(7):
            column = [taps[(6 - i) * 7 + 6 - j if flip else i * 7 + j][None] for i in range(7)]

            @pl.loop(span[0] // 16, span[1] // 16)
            def _(c):
                q = pl.ds(c * 2, 2)
                sums = [acc[p, q] if j else None for p in range(H)]
                for r in range(H + 6):
                    cells = xs[j, r, q]
                    for p in range(H):
                        i = r - p
                        if 0 <= i < 7:
                            term = cells * column[i]
                            sums[p] = term if sums[p] is None else sums[p] + term
                for p in range(H):
                    acc[p, q] = sums[p]

    def x_seg(k):
        @pl.when(home)
        def _():
            kept(*x_args(k)).wait()

        @pl.when(away)
        def _():
            moved(*x_args(k)).wait_recv()

        halo_start(*x_side, segs[k], k)
        lo, hi = segs[k]
        widen(xo[:, lo:hi], 3, lo)

    def x_halo(k):
        halo_arrive(*x_side, segs[k], k)
        lo, hi = segs[k]
        widen(x_top[:, lo:hi], 0, lo)
        widen(x_bot[:, lo:hi], H + 3, lo)

    def masks():
        @pl.when(home)
        def _():
            kept(*mask_args).wait()

        @pl.when(away)
        def _():
            moved(*mask_args).wait()

        mpad[...] = jnp.zeros_like(mpad)
        mpad[0:H, 0:W] = mbuf[...].astype(F32)
        flags = mpad[...].astype(BF16)
        lines = lax.broadcasted_iota(jnp.int32, (mpad.shape[0], C), 0)
        for p in range(H):
            pick = jnp.where(lines == p, 1.0, 0.0).astype(BF16)
            ocean_v[p] = lax.dot_general(
                flags, pick, (((0,), (0,)), ((), ())), preferred_element_type=F32
            ).astype(BF16)

    def rowsum(value):
        return jnp.sum(value, axis=0, keepdims=True)

    def give_back(src, dst, k):
        return remote(src, dst, back_send.at[k], back_recv.at[k], diag)

    def put(src, dst, k):
        return pltpu.make_async_copy(src, dst, back_local.at[k])

    def returned(src, dst, k):
        @pl.when(home)
        def _():
            put(src, dst, k).start()

        @pl.when(away)
        def _():
            give_back(src, dst, k).start()

    def cells(k):
        lo, hi = chunks[k]
        return slice(H * lo, H * hi)

    def ocean_of(k):
        lo, hi = chunks[k]
        return ocean_v[:, lo:hi].astype(F32).reshape(H * (hi - lo), C)

    def forward(k):
        lo, hi = chunks[k]
        size = H * (hi - lo)
        at = cells(k)
        conv_out = acc[:, lo // 8 : hi // 8].reshape(size, C) + conv_bias_ref[...]
        dev = conv_out - jnp.mean(conv_out, axis=-1, keepdims=True)
        rstd = lax.rsqrt(jnp.mean(dev * dev, axis=-1, keepdims=True) + EPSILON)
        unit = dev * rstd
        rstd_v[at] = jnp.broadcast_to(rstd, (size, 128))
        gf[at] = unit
        normed[at] = (unit * gain_ref[...] + nbias_ref[...]).astype(BF16)
        hid[0:size] = jnp.dot(normed[at], w_in_ref[...], preferred_element_type=F32)

        @pl.loop(0, size // 16)
        def _(c):
            q = pl.ds(pl.multiple_of(c * 16, 16), 16)
            to = pl.ds(pl.multiple_of(H * lo + c * 16, 16), 16)
            h = hid[q] + b_in_ref[...]
            h2 = h * h
            th = jnp.tanh(h * (h2 * (ROOT_TERM * CUBIC) + ROOT_TERM))
            half = 0.5 * th + 0.5
            a = h * half
            act[to] = a.astype(BF16)
            slope_v[to] = half + (a - a * th) * (h2 * (3.0 * CUBIC * ROOT_TERM) + ROOT_TERM)

        mixed = jnp.dot(act[at], w_out_ref[...], preferred_element_type=F32) + b_out_ref[...]
        mixed_v[at] = mixed
        change = (ocean_of(k) * ls_ref[...] * mixed).reshape(H, hi - lo, C)
        out_v[:, lo:hi] = (xo[:, lo:hi].astype(F32) + change).astype(BF16)
        returned(chunk(out_v, k), chunk(out_ref, k), k)

    for k in range(3):
        x_seg(k)
    masks()
    bsum[...] = jnp.zeros_like(bsum)
    chan[...] = jnp.zeros_like(chan)
    for copy in load_w:
        copy.wait()
    x_halo(0)
    wrap_left()
    for k in range(K):
        x_halo(k + 1)
        if k == 0:
            wrap_right()
        spread(chunks[k])
        conv(chunks[k], False)
        forward(k)
        if k == 0:

            @pl.when(away)
            def _():
                for q in range(N):
                    moved(*x_args(q)).wait_send()
                for q in range(K):
                    moved(*cot_args(q)).start()

            for q in range(3, N):
                x_seg(q)

    for k in range(K):

        @pl.when(home)
        def _():
            kept(*cot_args(k)).wait()

        @pl.when(away)
        def _():
            moved(*cot_args(k)).wait()

        lo, hi = chunks[k]
        size = H * (hi - lo)
        value = cotb[:, lo:hi].astype(F32).reshape(size, C)
        masked = ocean_of(k) * value
        grad_mixed = (ls_ref[...] * masked).astype(BF16)
        gmix[cells(k)] = grad_mixed
        chan[3:4] += rowsum(grad_mixed.astype(F32))
        chan[4:5] += rowsum(masked * mixed_v[cells(k)])

    T = part.shape[4]
    L = part.shape[6]
    tiles = 4 * m * T
    per = C // 16

    class Exchange:
        def __init__(self, w):
            self.w = w
            self.s = 4 * w
            self.z = 2 * (m - 1) * w

        def fill(self, tile):
            for k in range(tiles):
                part[self.w, k // (tiles // 2), k // (tiles // 4) % 2, k // T % m, k % T] = tile(
                    k
                ).astype(BF16)
            self.one().start()

        def one(self):
            w, s = self.w, self.s
            return remote(part.at[w, 1 - d], r1.at[w], send_sem.at[s], recv_sem.at[s], core)

        def two(self):
            w, s = self.w, self.s + 1
            return remote(r1.at[w, 1 - yy], r2.at[w], send_sem.at[s], recv_sem.at[s], beside)

        def three(self):
            w = self.w
            return [
                remote(
                    r2.at[w, lax.rem(zz + k, m)],
                    r3.at[w, k - 1],
                    z_send.at[self.z + k - 1],
                    z_recv.at[self.z + k - 1],
                    zpeer[k],
                )
                for k in range(1, m)
            ]

        def four(self):
            mine = whole.at[self.w, d, yy, zz]
            return [
                remote(
                    mine,
                    mine,
                    z_send.at[self.z + m - 2 + k],
                    z_recv.at[self.z + m - 2 + k],
                    zpeer[k],
                )
                for k in range(1, m)
            ]

        def five(self):
            mine = whole.at[self.w, d, yy]
            s = self.s + 2
            return remote(mine, mine, send_sem.at[s], recv_sem.at[s], beside)

        def six(self):
            mine = whole.at[self.w, d]
            s = self.s + 3
            return remote(mine, mine, send_sem.at[s], recv_sem.at[s], core)

        def after_one(self):
            w = self.w
            self.one().wait()
            r1[w] = (part[w, d].astype(F32) + r1[w].astype(F32)).astype(BF16)
            self.two().start()

        def after_two(self):
            w = self.w
            self.two().wait()
            r2[w] = (r1[w, yy].astype(F32) + r2[w].astype(F32)).astype(BF16)
            for copy in self.three():
                copy.start()

        def after_three(self):
            w = self.w
            for copy in self.three():
                copy.wait()
            total = r2[w, zz].astype(F32)
            for k in range(m - 1):
                total = total + r3[w, k].astype(F32)
            whole[w, d, yy, zz] = (total * scale).astype(BF16)
            for copy in self.four():
                copy.start()

        def after_four(self):
            for copy in self.four():
                copy.wait()
            self.five().start()

        def after_five(self):
            self.five().wait()
            self.six().start()

        def after_six(self):
            self.six().wait()

    ex_out = [Exchange(0), Exchange(1)]
    ex_in = [Exchange(2), Exchange(3)]

    d_out = lax.dot_general(
        gmix[...], act[...], (((0,), (0,)), ((), ())), preferred_element_type=F32
    ).T
    for e in range(2):
        ex_out[e].fill(lambda k: d_out[k * 16 : k * 16 + 16, e * L : e * L + L])

    def grads_hidden(k):
        lo, hi = chunks[k]
        size = H * (hi - lo)
        hid[0:size] = lax.dot_general(
            gmix[cells(k)], w_out_ref[...], (((1,), (1,)), ((), ())), preferred_element_type=F32
        )

        @pl.loop(0, size // 16)
        def _(c):
            q = pl.ds(pl.multiple_of(c * 16, 16), 16)
            to = pl.ds(pl.multiple_of(H * lo + c * 16, 16), 16)
            grad_hidden = (hid[q] * slope_v[to]).astype(BF16)
            gh[to] = grad_hidden
            wide = grad_hidden.astype(F32)
            bsum[...] += wide[0:8] + wide[8:16]

    def grads_conv(k):
        lo, hi = chunks[k]
        at = cells(k)
        grad_normed = lax.dot_general(
            gh[at], w_in_ref[...], (((1,), (1,)), ((), ())), preferred_element_type=F32
        )
        unit = gf[at]
        scaled = grad_normed * gain_ref[...]
        grad_conv = rstd_v[at][:, 0:1] * (
            scaled
            - jnp.mean(scaled, axis=-1, keepdims=True)
            - unit * jnp.mean(scaled * unit, axis=-1, keepdims=True)
        )
        rounded = grad_conv.astype(BF16).reshape(H, hi - lo, C)
        gb[:, lo:hi] = rounded
        halo_start(*g_side, chunks[k], N + k)
        wide = rounded.astype(F32)
        widen(wide, 3, lo)
        chan[0:1] += rowsum(wide.reshape(H * (hi - lo), C))
        chan[1:2] += rowsum(grad_normed * unit)
        chan[2:3] += rowsum(grad_normed)

    for k in range(K):
        grads_hidden(k)
        if k == 1:
            for ex in ex_out:
                ex.after_one()

    d_in = lax.dot_general(
        normed[...], gh[...], (((0,), (0,)), ((), ())), preferred_element_type=F32
    )

    def in_tile(e, k):
        rb, cb = k % per, k // per * C + e * L
        return d_in[rb * 16 : rb * 16 + 16, cb : cb + L]

    for e in range(2):
        ex_in[e].fill(lambda k: in_tile(e, k))
    for ex in ex_out:
        ex.after_two()

    for k in range(K):
        grads_conv(k)
        if k == 1:
            for ex in ex_in:
                ex.after_one()
    ex_in[0].after_two()
    for ex in ex_out:
        ex.after_three()

    for j in range(7):

        def tap_terms(c, sums):
            q = pl.ds(c * 2, 2)
            cells16 = pl.ds(pl.multiple_of(c * 16, 16), 16)
            grads = [gb[p, cells16].astype(F32).reshape(2, 8, C) for p in range(H)]
            sums = list(sums)
            for r in range(H + 6):
                cells = xs[j, r, q]
                for p in range(H):
                    i = r - p
                    if 0 <= i < 7:
                        term = cells * grads[p]
                        sums[i] = sums[i] + (term[0] + term[1])
            return tuple(sums)

        sums = lax.fori_loop(0, B // 2, tap_terms, tuple(jnp.zeros((8, C), F32) for _ in range(7)))
        for i in range(7):
            k = i * 7 + j
            sm[k // 32, k % 32 : k % 32 + 1] = rowsum(sums[i])
        if j == 1:
            ex_in[1].after_two()
        if j == 3:
            ex_in[0].after_three()
            for ex in ex_out:
                ex.after_four()
        if j == 4:
            ex_in[1].after_three()

    hidden_sum = rowsum(bsum[...])
    for k in range(HID // C):
        sm[1, 17 + k : 18 + k] = hidden_sum[:, k * C : k * C + C]
    sm[1, 21:26] = chan[0:5]
    sm[1, 26:32] = jnp.zeros((6, C), F32)

    small1 = remote(sm.at[1 - d], s1, send_sem.at[16], recv_sem.at[16], core)
    small1.start()

    for k in range(K):
        lo, hi = chunks[k]
        halo_arrive(*g_side, chunks[k], N + k)
        widen(g_top[:, lo:hi], 0, lo)
        widen(g_bot[:, lo:hi], H + 3, lo)
    wrap_left()
    wrap_right()
    small1.wait()
    s2[...] = sm[d] + s1[...]
    small2 = remote(s2, s3, send_sem.at[17], recv_sem.at[17], beside)
    small2.start()
    ex_in[0].after_four()
    for ex in ex_out:
        ex.after_five()

    zs = 8 * (m - 1) - 1

    def small3():
        return [
            remote(s5.at[zz], s5.at[zz], z_send.at[zs + k], z_recv.at[zs + k], zpeer[k])
            for k in range(1, m)
        ]

    for k in range(K):
        lo, hi = chunks[k]
        spread(chunks[k])
        conv(chunks[k], True)
        igrad_v[:, lo:hi] = (
            cotb[:, lo:hi].astype(F32) + acc[:, lo // 8 : hi // 8].reshape(H, hi - lo, C)
        ).astype(BF16)
        returned(chunk(igrad_v, k), chunk(igrad_ref, k), K + k)
        if k == 0:
            ex_in[1].after_four()
        if k == 2:
            for ex in ex_in:
                ex.after_five()
        if k == 1:
            small2.wait()
            s5[zz] = s2[...] + s3[...]
            for copy in small3():
                copy.start()

    for copy in small3():
        copy.wait()
    small_total = s5[0]
    for k in range(1, m):
        small_total = small_total + s5[k]
    s6[d] = small_total * scale
    small4 = remote(s6.at[d], s6.at[d], send_sem.at[18], recv_sem.at[18], core)
    small4.start()
    for k in range(N):
        halo_sent(*x_side, segs[k], k)
    for k in range(K):
        halo_sent(*g_side, chunks[k], N + k)
    for ex in ex_out:
        ex.after_six()
    last = [pltpu.make_async_copy(whole.at[0:2], wo_ref, w_local.at[0])]
    last[0].start()
    for ex in ex_in:
        ex.after_six()
    last.append(pltpu.make_async_copy(whole.at[2:4], wi_ref, w_local.at[1]))
    last[1].start()
    small4.wait()
    last.append(pltpu.make_async_copy(s6, rows_ref, w_local.at[2]))
    last[2].start()
    for k in range(2 * K):
        src, dst = ((out_v, out_ref), (igrad_v, igrad_ref))[k // K]
        pair = (chunk(src, k % K), chunk(dst, k % K), k)

        @pl.when(home)
        def _():
            put(*pair).wait()

        @pl.when(away)
        def _():
            give_back(*pair).wait()

    for copy in last:
        copy.wait()


def gather_kernel(wi_part, wo_part, rows_part, wi_ref, wo_ref, kgrad_ref, bgrad_ref, chan_ref):
    C = wi_ref.shape[0]
    HID = wi_ref.shape[1]
    per = C // 16
    _, _, _, m, T, _, L = wi_part.shape
    tiles = 4 * m * T
    rows = rows_part[...].reshape(64, C)
    for i in range(7):
        kgrad_ref[i] = rows[i * 7 : i * 7 + 7]
    for k in range(HID // C):
        bgrad_ref[0:1, k * C : k * C + C] = rows[49 + k : 50 + k]
    chan_ref[...] = rows[49 + HID // C : 54 + HID // C]
    for k in range(tiles):
        at = (k // (tiles // 2), k // (tiles // 4) % 2, k // T % m, k % T)
        rb, cb = k % per, k // per
        for e in range(2):
            wi_ref[rb * 16 : rb * 16 + 16, cb * C + e * L : cb * C + e * L + L] = wi_part[
                (e,) + at
            ].astype(F32)
            wo_ref[k * 16 : k * 16 + 16, e * L : e * L + L] = wo_part[(e,) + at].astype(F32)


def per_device(
    n,
    draws,
    inputs,
    land_mask,
    kernel,
    conv_bias,
    norm_gain,
    norm_bias,
    w_in,
    b_in,
    w_out,
    b_out,
    layer_scale,
    cotangent,
):
    _, H, W, C = inputs.shape
    HID = w_in.shape[1]
    Wp = (W + 15) // 16 * 16
    B = Wp // 8
    m = n // 2
    T = HID // 16 // (2 * n)
    scale = float(1.0 / (draws * H * n * W) ** 0.5)
    vm = pl.BlockSpec(memory_space=pltpu.VMEM)
    hbm = pl.BlockSpec(memory_space=pl.ANY)
    flat = H * Wp
    L = C // 2
    scratch = [
        ((H, Wp, C), BF16),
        ((3, Wp, C), BF16),
        ((3, Wp, C), BF16),
        ((H, Wp, C), BF16),
        ((H, W), jnp.int32),
        ((16, Wp), F32),
        ((H, Wp, C), BF16),
        ((49, 8, C), F32),
        ((C, HID), BF16),
        ((HID, C), BF16),
        ((H + 6, Wp + 16, C), F32),
        ((7, H + 6, B, 8, C), F32),
        ((H, B, 8, C), F32),
        ((flat // 4 + 256, HID), F32),
        ((flat, HID), F32),
        ((flat, HID), BF16),
        ((flat, HID), BF16),
        ((flat, C), BF16),
        ((flat, C), BF16),
        ((H, Wp, C), BF16),
        ((3, Wp, C), BF16),
        ((3, Wp, C), BF16),
        ((flat, C), F32),
        ((flat, 128), F32),
        ((flat, C), F32),
        ((H, Wp, C), BF16),
        ((H, Wp, C), BF16),
        ((8, HID), F32),
        ((8, C), F32),
        ((4, 2, 2, m, T, 16, L), BF16),
        ((4, 2, m, T, 16, L), BF16),
        ((4, m, T, 16, L), BF16),
        ((4, m - 1, T, 16, L), BF16),
        ((4, 2, 2, m, T, 16, L), BF16),
        ((2, 32, C), F32),
        ((32, C), F32),
        ((32, C), F32),
        ((32, C), F32),
        ((m, 32, C), F32),
        ((2, 32, C), F32),
    ]
    dma = pltpu.SemaphoreType.DMA
    output, input_grad, wi_part, wo_part, rows_part = pl.pallas_call(
        functools.partial(block_kernel, n, scale),
        out_shape=(
            jax.ShapeDtypeStruct((H, Wp, C), BF16),
            jax.ShapeDtypeStruct((H, Wp, C), BF16),
            jax.ShapeDtypeStruct((2, 2, 2, m, T, 16, L), BF16),
            jax.ShapeDtypeStruct((2, 2, 2, m, T, 16, L), BF16),
            jax.ShapeDtypeStruct((2, 32, C), F32),
        ),
        in_specs=[hbm, hbm, hbm, vm, vm, vm, vm, hbm, vm, hbm, vm, vm],
        out_specs=[hbm] * 5,
        scratch_shapes=[pltpu.VMEM(shape, dtype) for shape, dtype in scratch]
        + [
            dma((10,)),
            dma((10,)),
            dma((10,)),
            dma((8,)),
            dma((8,)),
            dma((8,)),
            dma((3,)),
            dma((18,)),
            dma((18,)),
            dma((19,)),
            dma((19,)),
            dma((9 * (m - 1),)),
            dma((9 * (m - 1),)),
        ],
        compiler_params=pltpu.CompilerParams(
            collective_id=0, has_side_effects=True, vmem_limit_bytes=60 * 1024 * 1024
        ),
        name="block",
    )(
        jnp.pad(inputs[0], ((0, 0), (0, Wp - W), (0, 0))),
        jnp.pad(cotangent[0], ((0, 0), (0, Wp - W), (0, 0))),
        land_mask,
        kernel,
        conv_bias[None],
        norm_gain[None],
        norm_bias[None],
        w_in,
        b_in[None],
        w_out,
        b_out[None],
        layer_scale[None],
    )
    w_in_grad, w_out_grad, kernel_grad, b_in_grad, channel = pl.pallas_call(
        gather_kernel,
        out_shape=(
            jax.ShapeDtypeStruct((C, HID), F32),
            jax.ShapeDtypeStruct((HID, C), F32),
            jax.ShapeDtypeStruct((7, 7, C), F32),
            jax.ShapeDtypeStruct((1, HID), F32),
            jax.ShapeDtypeStruct((5, C), F32),
        ),
        in_specs=[vm] * 3,
        out_specs=[vm] * 5,
        name="gather",
    )(wi_part, wo_part, rows_part)
    return (
        output[None, :, 0:W],
        input_grad[None, :, 0:W],
        kernel_grad,
        w_in_grad,
        w_out_grad,
        b_in_grad[0],
        channel,
    )


def solution(mesh):
    field = P(("group", "draw"), "tile", None, None)
    placed = (field, P("tile", None)) + (P(),) * 9 + (field,)
    return jax.shard_map(
        functools.partial(per_device, mesh.shape["tile"], mesh.shape["draw"]),
        mesh=mesh,
        in_specs=placed,
        out_specs=(
            field,
            field,
            P("group", None, None),
            P("group", None),
            P("group", None),
            P("group"),
            P("group", None),
        ),
        check_vma=False,
    )
```

time: 77.5 us -> 75 us (0.968)
  Pallas kernels: 71 us -> 67.3 us
  local copies, waits for them, and re-layouts: 5.65 us -> 6.77 us
    pallas_call x1, Pallas kernels: 68.4 us -> 64.6 us  [per_device(): pl.pallas_call(functools.partial(block_kernel, n, scale), out_shape=(jax....]
    squeeze x1 -> x0, local copies, waits for them, and re-layouts: 2.35 us -> none  [per_device(): cotangent[0]]
    pad x0 -> x2, local copies, waits for them, and re-layouts: none -> 1.69 us  [the longest x1 0.85 us: per_device(): jnp.pad(inputs[0], ((0, 0), (0, Wp - W), (0, 0)))]
    broadcast_in_dim x0 -> x1, local copies, waits for them, and re-layouts: none -> 1.3 us  [per_device(): input_grad[None, :, 0:W]]
    unnamed x4 -> x6, local copies, waits for them, and re-layouts: 3.29 us -> 3.78 us
where the time goes in v2:
time: 75 us; the launch traced here: 74.7 us
  Pallas kernels  67.3 us (90%)
  local copies, waits for them, and re-layouts  6.77 us (9%)
    pallas_call x1, Pallas kernels, per_device(): pl.pallas_call(functools.partial(block_kernel, n, scale), out_shape=(jax....  64.6 us
    unnamed x6, local copies, waits for them, and re-layouts  3.78 us
    pallas_call x1, Pallas kernels, per_device(): pl.pallas_call(gather_kernel, out_shape=(jax.ShapeDtypeStruct((C, HID), F...  2.61 us

profile of v2, /device:TPU:1, one launch (start us, length us, event | category | flops | bytes accessed | tf_op | source)
XLA Modules:
  0.0 74.7 jit_solution(1339413125103829608)
XLA Ops:
  0.6 1.1 %copy.26 = bf16[1,4,270,256]{3,2,1,0:T(8,128)(2,1)S(1)} copy(bf16[1,4,270,256]{3,1,2,0:T(4,128)(2,1)} %param.12) | data formatting | bytes 1105920 | tf_op args[0]
  1.8 0.0 copy-start
  1.8 0.8 %pad.7.x_ref = bf16[4,272,256]{2,1,0:T(8,128)(2,1)} pad(bf16[4,270,256]{2,1,0:T(8,128)(2,1)S(1)} %bitcast.18, bf16[]{:T(256)} %constant.2.clone.1), padding=0_0x0_2x0_0 | pad | bytes 1110018 | tf_op jit(solution)/shard_map/jit(_pad)/pad | solution.py:837
  2.6 0.4 copy-done
  3.0 0.1 copy.25
  3.1 0.8 %pad.8.cot_ref = bf16[4,272,256]{2,1,0:T(8,128)(2,1)} pad(bf16[4,270,256]{2,1,0:T(8,128)(2,1)S(1)} %bitcast.17, bf16[]{:T(256)} %constant.2.clone.1), padding=0_0x0_2x0_0 | pad | bytes 1110018 | tf_op jit(solution)/shard_map/jit(_pad)/pad | solution.py:838
  3.9 64.6 %block.1 = (bf16[4,272,256]{2,1,0:T(8,128)(2,1)}, bf16[4,272,256]{2,1,0:T(8,128)(2,1)}, bf16[2,2,2,4,4,16,128]{6,5,4,3,2,1,0:T(8,128)(2,1)}, bf16[2,2,2,4,4,16,128]{6,5,4,3,2,1,0:T(8,128)(2,1)}, f32[2,32,256]{2,1,0:T(8,128)}) custom-call(bf16[4,272,256]{2,1,0:T(8,128)(2,1)} %pad.7.x_ref, bf16[4,272,256]{2,1,0:T(8,128)(2,1)} %pad.8.cot_ref, ...), custom_call_target="tpu_custom_call" | custom-call | tf_op jit(solution)/shard_map/block/pallas_call | solution.py:805
  68.6 1.3 %slice_bitcast_fusion = (bf16[1,4,270,256]{3,2,1,0:T(8,128)(2,1)S(1)}, bf16[1,4,270,256]{3,2,1,0:T(8,128)(2,1)S(1)}) fusion(bf16[4,272,256]{2,1,0:T(8,128)(2,1)} %get-tuple-element.18, bf16[4,272,256]{2,1,0:T(8,128)(2,1)} %get-tuple-element.17), kind=kLoop, calls=%fused_computation.2 | loop fusion | bytes 2211840 | tf_op jit(solution)/shard_map/broadcast_in_dim | solution.py:865
  69.9 1.1 %copy.22 = bf16[1,4,270,256]{3,1,2,0:T(4,128)(2,1)} copy(bf16[1,4,270,256]{3,2,1,0:T(8,128)(2,1)S(1)} %get-tuple-element.34) | data formatting | bytes 1105920
  71.0 1.1 %copy.21 = bf16[1,4,270,256]{3,1,2,0:T(4,128)(2,1)} copy(bf16[1,4,270,256]{3,2,1,0:T(8,128)(2,1)S(1)} %get-tuple-element.35) | data formatting | bytes 1105920
  72.1 2.6 %gather.1 = (f32[256,1024]{1,0:T(8,128)}, f32[1024,256]{1,0:T(8,128)}, f32[7,7,256]{2,1,0:T(8,128)}, f32[1,1024]{1,0:T(1,128)}, f32[5,256]{1,0:T(8,128)}) custom-call(bf16[2,2,2,4,4,16,128]{6,5,4,3,2,1,0:T(8,128)(2,1)} %get-tuple-element.19.wi_part, bf16[2,2,2,4,4,16,128]{6,5,4,3,2,1,0:T(8,128)(2,1)} %get-tuple-element.20.wo_part, ...), custom_call_target="tpu_custom_call" | custom-call | tf_op jit(solution)/shard_map/gather/pallas_call | solution.py:850
Async XLA Ops:
  1.8 1.3 %copy-start = (bf16[1,4,270,256]{3,1,2,0:T(4,128)(2,1)S(1)}, bf16[1,4,270,256]{3,1,2,0:T(4,128)(2,1)}, u32[]{:S(2)}) copy-start(bf16[1,4,270,256]{3,1,2,0:T(4,128)(2,1)} %param.23) | copy-start | bytes 1658884

commit v3 on v2

--- a/solution.py
+++ b/solution.py
@@ -565,10 +565,9 @@
 
     for k in range(K):
         grads_hidden(k)
-        if k == 1:
-            for ex in ex_out:
-                ex.after_one()
-
+
+    for ex in ex_out:
+        ex.after_one()
     d_in = lax.dot_general(
         normed[...], gh[...], (((0,), (0,)), ((), ())), preferred_element_type=F32
     )
@@ -579,17 +578,14 @@
 
     for e in range(2):
         ex_in[e].fill(lambda k: in_tile(e, k))
-    for ex in ex_out:
-        ex.after_two()
-
     for k in range(K):
         grads_conv(k)
         if k == 1:
             for ex in ex_in:
                 ex.after_one()
+    for ex in ex_out:
+        ex.after_two()
     ex_in[0].after_two()
-    for ex in ex_out:
-        ex.after_three()
 
     for j in range(7):
 
@@ -615,10 +611,11 @@
             ex_in[1].after_two()
         if j == 3:
             ex_in[0].after_three()
-            for ex in ex_out:
-                ex.after_four()
         if j == 4:
             ex_in[1].after_three()
+        if j == 5:
+            for ex in ex_out:
+                ex.after_three()
 
     hidden_sum = rowsum(bsum[...])
     for k in range(HID // C):
@@ -641,8 +638,6 @@
     small2 = remote(s2, s3, send_sem.at[17], recv_sem.at[17], beside)
     small2.start()
     ex_in[0].after_four()
-    for ex in ex_out:
-        ex.after_five()
 
     zs = 8 * (m - 1) - 1
 
@@ -662,8 +657,12 @@
         returned(chunk(igrad_v, k), chunk(igrad_ref, k), K + k)
         if k == 0:
             ex_in[1].after_four()
+            for ex in ex_out:
+                ex.after_four()
         if k == 2:
             for ex in ex_in:
+                ex.after_five()
+            for ex in ex_out:
                 ex.after_five()
         if k == 1:
             small2.wait()
@@ -834,8 +833,8 @@
         ),
         name="block",
     )(
-        jnp.pad(inputs[0], ((0, 0), (0, Wp - W), (0, 0))),
-        jnp.pad(cotangent[0], ((0, 0), (0, Wp - W), (0, 0))),
+        jnp.concatenate([inputs[0], inputs[0, :, : Wp - W]], axis=1),
+        jnp.concatenate([cotangent[0], cotangent[0, :, : Wp - W]], axis=1),
         land_mask,
         kernel,
         conv_bias[None],

time: 75 us -> 74.2 us (0.989)
  local copies, waits for them, and re-layouts: 6.77 us -> 4.75 us
  other arithmetic: 0 us -> 1.69 us
    concatenate x0 -> x2, other arithmetic: none -> 1.69 us  [the longest x1 0.85 us: per_device(): jnp.concatenate([inputs[0], inputs[0, :, :Wp - W]], axis=1)]
    pad x2 -> x0, local copies, waits for them, and re-layouts: 1.69 us -> none  [the longest x1 0.85 us: per_device(): jnp.pad(inputs[0], ((0, 0), (0, Wp - W), (0, 0)))]
where the time goes in v3:
time: 74.2 us; the launch traced here: 74 us
  Pallas kernels  66.9 us (90%)
  local copies, waits for them, and re-layouts  4.75 us (6%)
  other arithmetic  1.69 us (2%)
    pallas_call x1, Pallas kernels, per_device(): pl.pallas_call(functools.partial(block_kernel, n, scale), out_shape=(jax....  64.3 us
    unnamed x6, local copies, waits for them, and re-layouts  3.44 us
    pallas_call x1, Pallas kernels, per_device(): pl.pallas_call(gather_kernel, out_shape=(jax.ShapeDtypeStruct((C, HID), F...  2.61 us

profile of v3, /device:TPU:1, one launch (start us, length us, event | category | flops | bytes accessed | tf_op | source)
XLA Modules:
  0.0 74.0 jit_solution(12253217910502214191)
XLA Ops:
  0.6 0.0 copy-start
  0.6 1.2 %copy.30 = bf16[1,4,270,256]{3,2,1,0:T(8,128)(2,1)S(1)} copy(bf16[1,4,270,256]{3,1,2,0:T(4,128)(2,1)} %param.12) | data formatting | bytes 1105920 | tf_op args[0]
  1.8 0.8 %pad_maximum_fusion.x_ref = bf16[4,272,256]{2,1,0:T(8,128)(2,1)} fusion(bf16[4,2,256]{2,1,0:T(2,128)(2,1)S(1)} %slice_bitcast_fusion.3, bf16[4,270,256]{2,1,0:T(8,128)(2,1)S(1)} %bitcast.21), kind=kLoop, calls=%fused_computation | loop fusion | flops 1114112 | bytes 1114112 | tf_op jit(solution)/shard_map/concatenate | solution.py:836
  2.7 0.0 copy-done
  2.7 0.1 copy.29
  2.8 0.8 %pad_maximum_fusion.1.cot_ref = bf16[4,272,256]{2,1,0:T(8,128)(2,1)} fusion(bf16[4,2,256]{2,1,0:T(2,128)(2,1)S(1)} %slice_bitcast_fusion.2, bf16[4,270,256]{2,1,0:T(8,128)(2,1)S(1)} %bitcast.22), kind=kLoop, calls=%fused_computation.1 | loop fusion | flops 1114112 | bytes 1114112 | tf_op jit(solution)/shard_map/concatenate | solution.py:837
  3.6 64.3 %block.1 = (bf16[4,272,256]{2,1,0:T(8,128)(2,1)}, bf16[4,272,256]{2,1,0:T(8,128)(2,1)}, bf16[2,2,2,4,4,16,128]{6,5,4,3,2,1,0:T(8,128)(2,1)}, bf16[2,2,2,4,4,16,128]{6,5,4,3,2,1,0:T(8,128)(2,1)}, f32[2,32,256]{2,1,0:T(8,128)}) custom-call(bf16[4,272,256]{2,1,0:T(8,128)(2,1)} %pad_maximum_fusion.x_ref, bf16[4,272,256]{2,1,0:T(8,128)(2,1)} %pad_maximum_fusion.1.cot_ref, ...), custom_call_target="tpu_custom_call" | custom-call | tf_op jit(solution)/shard_map/block/pallas_call | solution.py:804
  67.9 1.3 %slice_bitcast_fusion = (bf16[1,4,270,256]{3,2,1,0:T(8,128)(2,1)S(1)}, bf16[1,4,270,256]{3,2,1,0:T(8,128)(2,1)S(1)}) fusion(bf16[4,272,256]{2,1,0:T(8,128)(2,1)} %get-tuple-element.18, bf16[4,272,256]{2,1,0:T(8,128)(2,1)} %get-tuple-element.17), kind=kLoop, calls=%fused_computation.2 | loop fusion | bytes 2211840 | tf_op jit(solution)/shard_map/broadcast_in_dim | solution.py:864
  69.2 1.1 %copy.24 = bf16[1,4,270,256]{3,1,2,0:T(4,128)(2,1)} copy(bf16[1,4,270,256]{3,2,1,0:T(8,128)(2,1)S(1)} %get-tuple-element.38) | data formatting | bytes 1105920
  70.3 1.1 %copy.23 = bf16[1,4,270,256]{3,1,2,0:T(4,128)(2,1)} copy(bf16[1,4,270,256]{3,2,1,0:T(8,128)(2,1)S(1)} %get-tuple-element.39) | data formatting | bytes 1105920
  71.4 2.6 %gather.1 = (f32[256,1024]{1,0:T(8,128)}, f32[1024,256]{1,0:T(8,128)}, f32[7,7,256]{2,1,0:T(8,128)}, f32[1,1024]{1,0:T(1,128)}, f32[5,256]{1,0:T(8,128)}) custom-call(bf16[2,2,2,4,4,16,128]{6,5,4,3,2,1,0:T(8,128)(2,1)} %get-tuple-element.19.wi_part, bf16[2,2,2,4,4,16,128]{6,5,4,3,2,1,0:T(8,128)(2,1)} %get-tuple-element.20.wo_part, ...), custom_call_target="tpu_custom_call" | custom-call | tf_op jit(solution)/shard_map/gather/pallas_call | solution.py:849
  (2 shorter events, 0.0 us)
Async XLA Ops:
  0.6 2.1 %copy-start = (bf16[1,4,270,256]{3,1,2,0:T(4,128)(2,1)S(1)}, bf16[1,4,270,256]{3,1,2,0:T(4,128)(2,1)}, u32[]{:S(2)}) copy-start(bf16[1,4,270,256]{3,1,2,0:T(4,128)(2,1)} %param.23) | copy-start | bytes 1658884
